TPU v7x, 512 devices: a whole 4x8x8 slice. The times are simulated.
512 devices in a mesh: seq: 128 (over z, y, core), ch: 4 (over x).
Axes of the slice: x: 4, y: 8, z: 8, core: 2. Of those that a mesh axis runs over, the one named last changes fastest.
Arguments:
- gate: bfloat16 [16384, 8, 512], P('seq', 'ch'), may hold values from -6 to 6
- value: bfloat16 [16384, 8, 512], P('seq', 'ch'), may hold values from -6 to 6
- filt: bfloat16 [16384, 512], P('seq'), may hold values from -6 to 6
- cotangent: bfloat16 [16384, 8, 512], P('seq', 'ch'), may hold values from -6 to 6
Outputs:
- out: bfloat16 [16384, 8, 512], P('seq', 'ch')
- gate_grad: bfloat16 [16384, 8, 512], P('seq', 'ch')
- value_grad: bfloat16 [16384, 8, 512], P('seq', 'ch')
- filt_grad: bfloat16 [16384, 512], P('seq', 'ch')
All inputs are finite; a program needn't handle non-finite values.
Results may differ from a plain program's by a relative error of at most 0.0011.
Values sent between devices are 32-bit elements; how exact they have to be, the bound alone decides.
No kernel may reach another device: no remote copies, remote signals or barrier semaphores. Data moves between devices by JAX's collectives and lax.ppermute only.
A program may use at most 64 MiB of HBM per device.

v0:
```python
import math

import jax
import jax.numpy as jnp
import numpy as np
from jax import lax
from jax.experimental import pallas as pl
from jax.experimental.pallas import tpu as pltpu
from jax.sharding import PartitionSpec as P

F32 = jnp.float32
BF16 = jnp.bfloat16
VMEM = pl.BlockSpec(memory_space=pltpu.VMEM)
LIMIT = 48 * 1024 * 1024


def two_parts(table):
    high = table.astype(jnp.bfloat16)
    low = (table - high.astype(np.float64)).astype(jnp.bfloat16)
    return high, low


def make_tables(rows, blocks):
    kappa = np.arange(blocks)[:, None]
    block = np.arange(blocks)[None, :]
    angle = math.pi / (2 * blocks) * ((2 * kappa + 1) * block % (4 * blocks))
    stage1 = np.concatenate([np.cos(angle), -np.sin(angle)], axis=0)
    row = np.arange(rows)[None, :]
    turn = math.pi / (2 * rows * blocks) * ((2 * kappa + 1) * row % (4 * rows * blocks))
    k = np.arange(rows)[None, :]
    angle = 2 * math.pi / rows * (np.arange(rows)[:, None] * k % rows)
    cos, sin = np.cos(angle), np.sin(angle)
    stage2 = np.concatenate(
        [np.concatenate([cos, -sin], axis=1), np.concatenate([sin, cos], axis=1)], axis=0
    )
    back1 = stage1.T / (rows * blocks)
    back2 = stage2.T
    parts = []
    for table in (stage1, stage2, back1, back2):
        parts.extend(two_parts(table))
    return tuple(parts) + (np.cos(turn).astype(np.float32), np.sin(turn).astype(np.float32))


def split(x):
    high = x.astype(BF16)
    return high, (x - high.astype(F32)).astype(BF16)


def dot(a, b):
    return jnp.dot(a, b, preferred_element_type=F32)


def left_dot(high, low, x):
    x_high, x_low = split(x)
    return dot(high, x_high) + dot(high, x_low) + dot(low, x_high)


def right_dot(x, high, low):
    x_high, x_low = split(x)
    return dot(x_high, high) + dot(x_low, high) + dot(x_high, low)


def lanes(x, index, width=128):
    return x[:, index * width:(index + 1) * width]


def transform(x_ref, first, count, stride, exact, w_high, w_low, m_high, m_low, tc, ts):
    blocks = w_high.shape[1]
    columns = [x_ref[pl.ds(first + c, blocks, stride=stride), :] for c in range(count)]
    x = jnp.concatenate(columns, axis=1)
    if exact:
        x = x.astype(BF16)
        a = dot(w_high[...], x) + dot(w_low[...], x)
    else:
        a = left_dot(w_high[...], w_low[...], x)
    re, im = a[:blocks], a[blocks:]
    pieces = []
    for c in range(count):
        cr, ci = lanes(re, c), lanes(im, c)
        pieces.append(
            jnp.concatenate([cr * tc + ci * ts, ci * tc - cr * ts], axis=1)
        )
    return right_dot(jnp.concatenate(pieces, axis=0), m_high[...], m_low[...])


def inverse(spectra, w_high, w_low, m_high, m_low, tc, ts):
    blocks = w_high.shape[0]
    count = spectra.shape[0] // blocks
    c = right_dot(spectra, m_high[...], m_low[...])
    pieces = []
    for i in range(count):
        part = c[i * blocks:(i + 1) * blocks]
        cr, ci = lanes(part, 0), lanes(part, 1)
        pieces.append(
            jnp.concatenate([cr * tc - ci * ts, cr * ts + ci * tc], axis=0)
        )
    return left_dot(w_high[...], w_low[...], jnp.concatenate(pieces, axis=1))


def pack_kernel(group, parts, gate_ref, value_ref, cot_ref, filt_ref, out_ref):
    rows = gate_ref.shape[0]
    stride = out_ref.shape[0] // rows
    scale = 1.0 / math.sqrt(rows * rows)
    width = group * parts
    for c in range(parts):
        out_ref[pl.ds(width + c, rows, stride=stride), :] = (
            lanes(filt_ref, c).astype(F32) * scale
        ).T
    for c in range(width):
        out_ref[pl.ds(c, rows, stride=stride), :] = lanes(value_ref, c).astype(F32).T
    for c in range(width):
        gated = lanes(gate_ref, c).astype(F32) * lanes(cot_ref, c).astype(F32)
        out_ref[pl.ds(width + parts + c, rows, stride=stride), :] = gated.T


def spectra_kernel(
    group, parts, scale, x_ref, w1h, w1l, m2h, m2l, b1h, b1l, n2h, n2l, tcr, tsr,
    hs_ref, vs_ref, gs_ref, dh_ref,
):
    blocks = w1h.shape[1]
    stride = x_ref.shape[0] // blocks
    width = group * parts
    tc, ts = tcr[...], tsr[...]
    fwd = (w1h, w1l, m2h, m2l, tc, ts)
    vs_ref[...] = transform(x_ref, 0, width, stride, True, *fwd)
    gs_ref[...] = transform(x_ref, width + parts, width, stride, False, *fwd)
    pieces = []
    for q in range(parts):
        total_re = total_im = 0.0
        for s in range(group):
            at = pl.ds((s * parts + q) * blocks, blocks)
            v, g = vs_ref[at, :], gs_ref[at, :]
            vr, vi, gr, gi = lanes(v, 0), lanes(v, 1), lanes(g, 0), lanes(g, 1)
            total_re += gr * vr + gi * vi
            total_im += gi * vr - gr * vi
        pieces.append(jnp.concatenate([total_re, total_im], axis=1))
    dh = inverse(jnp.concatenate(pieces, axis=0), b1h, b1l, n2h, n2l, tc, ts)
    for q in range(parts):
        dh_ref[q] = lanes(dh, q) * scale
    hs_ref[...] = transform(x_ref, width, parts, stride, True, *fwd)


def products_kernel(
    group, parts, hs_ref, vs_ref, gs_ref, b1h, b1l, n2h, n2l, tcr, tsr, out_ref
):
    blocks = b1h.shape[0]
    stride = out_ref.shape[0] // blocks
    width = group * parts
    inv = (b1h, b1l, n2h, n2l, tcr[...], tsr[...])
    for which, ref in enumerate((vs_ref, gs_ref)):
        sign = 1.0 if which == 0 else -1.0
        pieces = []
        for c in range(width):
            x = ref[pl.ds(c * blocks, blocks), :]
            h = hs_ref[pl.ds((c % parts) * blocks, blocks), :]
            xr, xi, hr, hi = lanes(x, 0), lanes(x, 1), lanes(h, 0), lanes(h, 1) * sign
            pieces.append(jnp.concatenate([xr * hr - xi * hi, xr * hi + xi * hr], axis=1))
        y = inverse(jnp.concatenate(pieces, axis=0), *inv)
        for c in range(width):
            out_ref[pl.ds(which * width + c, blocks, stride=stride), :] = lanes(y, c)


def merge_kernel(dh_ref, big_ref, out_ref):
    parts, blocks, rows = dh_ref.shape
    stride = out_ref.shape[0] // blocks
    out_ref[...] = big_ref[...]
    total = dh_ref[0]
    for q in range(1, parts):
        total += dh_ref[q]
    out_ref[pl.ds(stride - 1, blocks, stride=stride), :] = total


def unpack_kernel(
    group, parts, x_ref, gate_ref, cot_ref, out_ref, gate_grad_ref, value_grad_ref, filt_ref
):
    rows = gate_ref.shape[0]
    stride = x_ref.shape[0] // rows
    width = group * parts
    for c in range(width):
        at = pl.ds(c * 128, 128)
        conv = x_ref[pl.ds(c, rows, stride=stride), :].T
        out_ref[:, at] = (gate_ref[:, at].astype(F32) * conv).astype(BF16)
        gate_grad_ref[:, at] = (cot_ref[:, at].astype(F32) * conv).astype(BF16)
        value_grad_ref[:, at] = x_ref[pl.ds(width + c, rows, stride=stride), :].T.astype(BF16)
    filt_ref[...] = x_ref[pl.ds(2 * width, rows, stride=stride), :].T.astype(BF16)


def call(body, outs, *args, **kw):
    return pl.pallas_call(
        body,
        out_shape=outs,
        in_specs=[VMEM] * len(args),
        out_specs=jax.tree.map(lambda _: VMEM, outs),
        compiler_params=pltpu.CompilerParams(vmem_limit_bytes=LIMIT),
        **kw,
    )(*args)


def exchange(x, blocks):
    flat = x.reshape(blocks, -1)
    return lax.all_to_all(flat, "seq", split_axis=0, concat_axis=0, tiled=True).reshape(x.shape)


def per_device(gate, value, filt, cotangent):
    rows, group, filters = value.shape
    blocks = lax.axis_size("seq")
    parts = filters // blocks
    width = group * parts
    w1h, w1l, m2h, m2l, b1h, b1l, n2h, n2l, tc, ts = make_tables(rows, blocks)
    gate = gate.reshape(rows, group * filters)
    value = value.reshape(rows, group * filters)
    cotangent = cotangent.reshape(rows, group * filters)

    def shape(*dims, dtype=F32):
        return jax.ShapeDtypeStruct(dims, dtype)

    sent = call(
        lambda *refs: pack_kernel(group, parts, *refs),
        shape(blocks * (2 * width + parts), rows),
        gate, value, cotangent, filt,
    )
    held = exchange(sent, blocks)
    scale = 1.0 / math.sqrt(rows * blocks)
    hs, vs, gs, dh = call(
        lambda *refs: spectra_kernel(group, parts, scale, *refs),
        (
            shape(parts * blocks, 2 * rows),
            shape(width * blocks, 2 * rows),
            shape(width * blocks, 2 * rows),
            shape(parts, blocks, rows),
        ),
        held, w1h, w1l, m2h, m2l, b1h, b1l, n2h, n2l, tc, ts,
    )
    dh = lax.all_to_all(dh, "ch", split_axis=0, concat_axis=0, tiled=True)
    big = call(
        lambda *refs: products_kernel(group, parts, *refs),
        shape(blocks * (2 * width + 1), rows),
        hs, vs, gs, b1h, b1l, n2h, n2l, tc, ts,
    )
    big = call(
        merge_kernel,
        shape(blocks * (2 * width + 1), rows),
        dh, big,
    )
    back = exchange(big, blocks)
    token = shape(rows, group * filters, dtype=BF16)
    out, gate_grad, value_grad, filt_grad = call(
        lambda *refs: unpack_kernel(group, parts, *refs),
        (token, token, token, shape(rows, blocks, dtype=BF16)),
        back, gate, cotangent,
    )
    full = (rows, group, filters)
    return out.reshape(full), gate_grad.reshape(full), value_grad.reshape(full), filt_grad


def solution(mesh):
    return jax.shard_map(
        per_device,
        mesh=mesh,
        in_specs=(P("seq", "ch", None), P("seq", "ch", None), P("seq", None), P("seq", "ch", None)),
        out_specs=(
            P("seq", "ch", None),
            P("seq", "ch", None),
            P("seq", "ch", None),
            P("seq", "ch"),
        ),
        check_vma=False,
    )
```

profile of v0, /device:TPU:1, one launch (start us, length us, event | category | flops | bytes accessed | tf_op | source)
XLA Modules:
  0.0 116.8 jit_solution(8812202740503610059)
XLA Ops:
  0.7 1.0 copy.20
  1.7 1.0 copy.21
  2.7 0.3 shard_map.165
  3.1 0.0 copy-start.2
  3.1 0.0 copy-start.3
  3.1 0.0 copy-start.7
  3.1 0.0 copy-start.8
  3.1 0.0 copy-start.9
  3.1 0.0 copy-start.11
  3.2 54.4 %all_to_all.23 = f32[128,1,2560]{2,1,0:T(1,128)S(1)} all-to-all(f32[128,1,2560]{2,1,0:T(1,128)S(1)} %bitcast.11), channel_id=1, replica_groups=mesh['seq'=128,'ch'=4] {'seq'}, dimensions={0} | all-to-all | bytes 2621440 | tf_op jit(solution)/shard_map/all_to_all | solution.py:201
  57.7 3.7 %shard_map.166 = (f32[512,256]{1,0:T(8,128)S(1)}, f32[1024,256]{1,0:T(8,128)S(1)}, f32[1024,256]{1,0:T(8,128)S(1)}, f32[4,128,128]{2,1,0:T(8,128)}) custom-call(f32[2560,128]{1,0:T(8,128)S(1)} %bitcast.10, bf16[256,128]{1,0:T(8,128)(2,1)S(1)} %copy-done.14, bf16[256,128]{1,0:T(8,128)(2,1)S(1)} %copy-done.13, bf16[256,256]{1,0:T(8,128)(2,1)S(1)} %copy-done.12, ...), custom_call_target="tpu_custom_call" | custom-call | tf_op jit(solution)/shard_map/pallas_call | solution.py:189
  61.4 1.0 copy-done
  62.4 0.8 copy-done.4
  63.2 4.0 %all-to-all-start.1 = ((f32[4,128,128]{2,1,0:T(8,128)}), f32[4,128,128]{2,1,0:T(8,128)S(1)}, u32[]{:S(2)}, u32[]{:S(2)}) async-start(f32[4,128,128]{2,1,0:T(8,128)} %get-tuple-element.12), calls=%async_computation.1 | async-start | bytes 524288 | tf_op jit(solution)/shard_map/all_to_all | solution.py:234
  67.2 1.2 %copy-done.1 = f32[1024,256]{1,0:T(8,128)S(1)} copy-done((f32[1024,256]{1,0:T(8,128)S(1)}, f32[1024,256]{1,0:T(8,128)}, u32[]{:S(2)}) %copy-start.1) | copy-done | bytes 1048600
  68.4 1.0 copy-done.5
  69.5 2.7 %shard_map.167.big_ref = f32[2176,128]{1,0:T(8,128)S(1)} custom-call(f32[512,256]{1,0:T(8,128)S(1)} %copy-done.5, f32[1024,256]{1,0:T(8,128)S(1)} %get-tuple-element.14.refs_1_, f32[1024,256]{1,0:T(8,128)S(1)} %copy-done.1, bf16[128,256]{1,0:T(8,128)(2,1)S(1)} %copy-done.9, bf16[128,256]{1,0:T(8,128)(2,1)S(1)} %copy-done.8, bf16[256,256]{1,0:T(8,128)(2,1)S(1)} %copy-done.3, ...), custom_call_target="tpu_custom_call" | custom-call | tf_op jit(solution)/shard_map/pallas_call | solution.py:189
  72.1 0.8 all-to-all-done.1.dh_ref
  73.0 0.1 shard_map.168
  73.1 40.2 %all_to_all.24 = f32[128,1,2176]{2,1,0:T(1,128)S(1)} all-to-all(f32[128,1,2176]{2,1,0:T(1,128)S(1)} %bitcast.12), channel_id=1, replica_groups=mesh['seq'=128,'ch'=4] {'seq'}, dimensions={0} | all-to-all | bytes 2228224 | tf_op jit(solution)/shard_map/all_to_all | solution.py:201
  113.2 0.9 shard_map.169
  114.1 0.9 reshape.47
  115.0 0.9 reshape.48
  115.9 0.9 reshape.49
  (23 shorter events, 0.1 us)
Async XLA Ops:
  0.6 2.0 %copy-start.15 = (bf16[128,2,512]{2,1,0:T(2,128)(2,1)S(1)}, bf16[128,2,512]{2,1,0:T(2,128)(2,1)}, u32[]{:S(2)}) copy-start(bf16[128,2,512]{2,1,0:T(2,128)(2,1)} %param.17) | copy-start | bytes 786436
  0.6 2.1 %copy-start.10 = (bf16[128,512]{1,0:T(8,128)(2,1)S(1)}, bf16[128,512]{1,0:T(8,128)(2,1)}, u32[]{:S(2)}) copy-start(bf16[128,512]{1,0:T(8,128)(2,1)} %refs_3_.3) | copy-start | bytes 393220
  3.1 54.5 %copy-start.2 = (bf16[256,256]{1,0:T(8,128)(2,1)S(1)}, bf16[256,256]{1,0:T(8,128)(2,1)}, u32[]{:S(2)}) copy-start(bf16[256,256]{1,0:T(8,128)(2,1)} %constant.27.clone.refs_8_.refs_6_) | copy-start | bytes 393220
  3.1 54.5 %copy-start.3 = (bf16[256,256]{1,0:T(8,128)(2,1)S(1)}, bf16[256,256]{1,0:T(8,128)(2,1)}, u32[]{:S(2)}) copy-start(bf16[256,256]{1,0:T(8,128)(2,1)} %constant.26.clone.refs_7_.refs_5_) | copy-start | bytes 393220
  3.1 54.5 %copy-start.6 = (f32[128,128]{1,0:T(8,128)S(1)}, f32[128,128]{1,0:T(8,128)}, u32[]{:S(2)}) copy-start(f32[128,128]{1,0:T(8,128)} %constant.29.clone.refs_10_.refs_8_) | copy-start | bytes 196612
  3.1 54.5 %copy-start.7 = (f32[128,128]{1,0:T(8,128)S(1)}, f32[128,128]{1,0:T(8,128)}, u32[]{:S(2)}) copy-start(f32[128,128]{1,0:T(8,128)} %constant.28.clone.refs_9_.refs_7_) | copy-start | bytes 196612
  3.1 54.5 %copy-start.8 = (bf16[128,256]{1,0:T(8,128)(2,1)S(1)}, bf16[128,256]{1,0:T(8,128)(2,1)}, u32[]{:S(2)}) copy-start(bf16[128,256]{1,0:T(8,128)(2,1)} %constant.25.clone.refs_6_.refs_4_) | copy-start | bytes 196612
  3.1 54.5 %copy-start.9 = (bf16[128,256]{1,0:T(8,128)(2,1)S(1)}, bf16[128,256]{1,0:T(8,128)(2,1)}, u32[]{:S(2)}) copy-start(bf16[128,256]{1,0:T(8,128)(2,1)} %constant.24.clone.refs_5_.refs_3_) | copy-start | bytes 196612
  3.1 54.5 %copy-start.11 = (bf16[256,256]{1,0:T(8,128)(2,1)S(1)}, bf16[256,256]{1,0:T(8,128)(2,1)}, u32[]{:S(2)}) copy-start(bf16[256,256]{1,0:T(8,128)(2,1)} %constant.23.clone.refs_4_) | copy-start | bytes 393220
  3.2 54.5 %copy-start.12 = (bf16[256,256]{1,0:T(8,128)(2,1)S(1)}, bf16[256,256]{1,0:T(8,128)(2,1)}, u32[]{:S(2)}) copy-start(bf16[256,256]{1,0:T(8,128)(2,1)} %constant.22.clone.refs_3_) | copy-start | bytes 393220
  3.2 54.5 %copy-start.13 = (bf16[256,128]{1,0:T(8,128)(2,1)S(1)}, bf16[256,128]{1,0:T(8,128)(2,1)}, u32[]{:S(2)}) copy-start(bf16[256,128]{1,0:T(8,128)(2,1)} %constant.21.clone.refs_2_) | copy-start | bytes 196612
  3.2 54.5 %copy-start.14 = (bf16[256,128]{1,0:T(8,128)(2,1)S(1)}, bf16[256,128]{1,0:T(8,128)(2,1)}, u32[]{:S(2)}) copy-start(bf16[256,128]{1,0:T(8,128)(2,1)} %constant.20.clone.refs_1_) | copy-start | bytes 196612
  61.4 1.0 copy-start
  62.4 0.8 copy-start.4
  63.2 9.8 %all-to-all-start.1 = ((f32[4,128,128]{2,1,0:T(8,128)}), f32[4,128,128]{2,1,0:T(8,128)S(1)}, u32[]{:S(2)}, u32[]{:S(2)}) async-start(f32[4,128,128]{2,1,0:T(8,128)} %get-tuple-element.12), calls=%async_computation.1 | async-start | bytes 524288 | tf_op jit(solution)/shard_map/all_to_all | solution.py:234
  67.2 1.2 %copy-start.1 = (f32[1024,256]{1,0:T(8,128)S(1)}, f32[1024,256]{1,0:T(8,128)}, u32[]{:S(2)}) copy-start(f32[1024,256]{1,0:T(8,128)} %copy-done) | copy-start | bytes 3145732
  68.4 1.0 copy-start.5
where the time goes:
time: 117 us
  blocking collectives  94.6 us (81%)
  local copies, waits for them, and re-layouts  8.81 us (8%)
  Pallas kernels  7.68 us (7%)
  starting transfers between devices  4.01 us (3%)
    all_to_all x2, blocking collectives, exchange(): lax.all_to_all(flat, 'seq', split_axis=0, concat_axis=0, tiled=True)  94.6 us
    pallas_call x5, Pallas kernels, call(): pl.pallas_call(body, out_shape=outs, in_specs=[VMEM] * len(args), out_spe...  7.68 us
    unnamed x35, local copies, waits for them, and re-layouts  6.17 us
    all_to_all x1, starting transfers between devices, per_device(): dh = lax.all_to_all(dh, 'ch', split_axis=0, concat_axis=0, tiled=True)  4.01 us
  transfers between devices with their start and end apart: 1, of which 1 were waited for; matrix products, arithmetic and copies ran while one was open for 0% of the time, Pallas kernels for 2%

commit v1 on v0

--- a/solution.py
+++ b/solution.py
@@ -11,7 +11,7 @@
 F32 = jnp.float32
 BF16 = jnp.bfloat16
 VMEM = pl.BlockSpec(memory_space=pltpu.VMEM)
-LIMIT = 48 * 1024 * 1024
+LIMIT = 24 * 1024 * 1024
 
 
 def two_parts(table):
@@ -64,15 +64,16 @@
     return x[:, index * width:(index + 1) * width]
 
 
-def transform(x_ref, first, count, stride, exact, w_high, w_low, m_high, m_low, tc, ts):
-    blocks = w_high.shape[1]
+def transform(x_ref, first, count, stride, exact, pair, high, m_high, m_low, tc, ts):
+    blocks = high.shape[1]
     columns = [x_ref[pl.ds(first + c, blocks, stride=stride), :] for c in range(count)]
     x = jnp.concatenate(columns, axis=1)
     if exact:
         x = x.astype(BF16)
-        a = dot(w_high[...], x) + dot(w_low[...], x)
+        a = dot(pair[...], jnp.concatenate([x, x], axis=0))
     else:
-        a = left_dot(w_high[...], w_low[...], x)
+        x, low = split(x)
+        a = dot(pair[...], jnp.concatenate([x, x], axis=0)) + dot(high[...], low)
     re, im = a[:blocks], a[blocks:]
     pieces = []
     for c in range(count):
@@ -97,38 +98,38 @@
     return left_dot(w_high[...], w_low[...], jnp.concatenate(pieces, axis=1))
 
 
-def pack_kernel(group, parts, gate_ref, value_ref, cot_ref, filt_ref, out_ref):
-    rows = gate_ref.shape[0]
+def pack_kernel(width, parts, gate_ref, value_ref, cot_ref, filt_ref, out_ref, v_ref, g_ref):
+    rows = filt_ref.shape[0]
     stride = out_ref.shape[0] // rows
     scale = 1.0 / math.sqrt(rows * rows)
-    width = group * parts
+    v_ref[...] = value_ref[...].astype(F32)
+    g_ref[...] = cot_ref[...].astype(F32) * gate_ref[...].astype(F32)
+    for c in range(width):
+        at = pl.ds(c, rows, stride=width)
+        out_ref[pl.ds(c, rows, stride=stride), :] = v_ref[at, :].T
+        out_ref[pl.ds(width + c, rows, stride=stride), :] = g_ref[at, :].T
     for c in range(parts):
-        out_ref[pl.ds(width + c, rows, stride=stride), :] = (
+        out_ref[pl.ds(2 * width + c, rows, stride=stride), :] = (
             lanes(filt_ref, c).astype(F32) * scale
         ).T
-    for c in range(width):
-        out_ref[pl.ds(c, rows, stride=stride), :] = lanes(value_ref, c).astype(F32).T
-    for c in range(width):
-        gated = lanes(gate_ref, c).astype(F32) * lanes(cot_ref, c).astype(F32)
-        out_ref[pl.ds(width + parts + c, rows, stride=stride), :] = gated.T
 
 
 def spectra_kernel(
-    group, parts, scale, x_ref, w1h, w1l, m2h, m2l, b1h, b1l, n2h, n2l, tcr, tsr,
-    hs_ref, vs_ref, gs_ref, dh_ref,
+    group, parts, scale, x_ref, pair, w1h, m2h, m2l, b1h, b1l, n2h, n2l, tcr, tsr,
+    dh_ref, vs_ref, gs_ref,
 ):
     blocks = w1h.shape[1]
     stride = x_ref.shape[0] // blocks
     width = group * parts
     tc, ts = tcr[...], tsr[...]
-    fwd = (w1h, w1l, m2h, m2l, tc, ts)
+    fwd = (pair, w1h, m2h, m2l, tc, ts)
     vs_ref[...] = transform(x_ref, 0, width, stride, True, *fwd)
-    gs_ref[...] = transform(x_ref, width + parts, width, stride, False, *fwd)
+    gs_ref[...] = transform(x_ref, width, width, stride, False, *fwd)
     pieces = []
     for q in range(parts):
         total_re = total_im = 0.0
         for s in range(group):
-            at = pl.ds((s * parts + q) * blocks, blocks)
+            at = pl.ds((q * group + s) * blocks, blocks)
             v, g = vs_ref[at, :], gs_ref[at, :]
             vr, vi, gr, gi = lanes(v, 0), lanes(v, 1), lanes(g, 0), lanes(g, 1)
             total_re += gr * vr + gi * vi
@@ -137,22 +138,27 @@
     dh = inverse(jnp.concatenate(pieces, axis=0), b1h, b1l, n2h, n2l, tc, ts)
     for q in range(parts):
         dh_ref[q] = lanes(dh, q) * scale
-    hs_ref[...] = transform(x_ref, width, parts, stride, True, *fwd)
 
 
 def products_kernel(
-    group, parts, hs_ref, vs_ref, gs_ref, b1h, b1l, n2h, n2l, tcr, tsr, out_ref
+    group, parts, x_ref, pair, w1h, m2h, m2l, b1h, b1l, n2h, n2l, tcr, tsr, out_ref
 ):
-    blocks = b1h.shape[0]
+    blocks = w1h.shape[1]
     stride = out_ref.shape[0] // blocks
     width = group * parts
-    inv = (b1h, b1l, n2h, n2l, tcr[...], tsr[...])
-    for which, ref in enumerate((vs_ref, gs_ref)):
+    tc, ts = tcr[...], tsr[...]
+    held = x_ref.shape[0] // blocks
+    fwd = (pair, w1h, m2h, m2l, tc, ts)
+    inv = (b1h, b1l, n2h, n2l, tc, ts)
+    spectra = transform(x_ref, 2 * width, parts, held, True, *fwd)
+    for which in range(2):
+        signal = transform(x_ref, which * width, width, held, which == 0, *fwd)
         sign = 1.0 if which == 0 else -1.0
         pieces = []
         for c in range(width):
-            x = ref[pl.ds(c * blocks, blocks), :]
-            h = hs_ref[pl.ds((c % parts) * blocks, blocks), :]
+            x = signal[c * blocks:(c + 1) * blocks]
+            q = c // group
+            h = spectra[q * blocks:(q + 1) * blocks]
             xr, xi, hr, hi = lanes(x, 0), lanes(x, 1), lanes(h, 0), lanes(h, 1) * sign
             pieces.append(jnp.concatenate([xr * hr - xi * hi, xr * hi + xi * hr], axis=1))
         y = inverse(jnp.concatenate(pieces, axis=0), *inv)
@@ -171,17 +177,19 @@
 
 
 def unpack_kernel(
-    group, parts, x_ref, gate_ref, cot_ref, out_ref, gate_grad_ref, value_grad_ref, filt_ref
+    width, x_ref, gate_ref, cot_ref, out_ref, gate_grad_ref, value_grad_ref, filt_ref,
+    conv_ref, grad_ref,
 ):
-    rows = gate_ref.shape[0]
+    rows = filt_ref.shape[0]
     stride = x_ref.shape[0] // rows
-    width = group * parts
     for c in range(width):
-        at = pl.ds(c * 128, 128)
-        conv = x_ref[pl.ds(c, rows, stride=stride), :].T
-        out_ref[:, at] = (gate_ref[:, at].astype(F32) * conv).astype(BF16)
-        gate_grad_ref[:, at] = (cot_ref[:, at].astype(F32) * conv).astype(BF16)
-        value_grad_ref[:, at] = x_ref[pl.ds(width + c, rows, stride=stride), :].T.astype(BF16)
+        at = pl.ds(c, rows, stride=width)
+        conv_ref[at, :] = x_ref[pl.ds(c, rows, stride=stride), :].T
+        grad_ref[at, :] = x_ref[pl.ds(width + c, rows, stride=stride), :].T
+    conv = conv_ref[...]
+    out_ref[...] = (gate_ref[...].astype(F32) * conv).astype(BF16)
+    gate_grad_ref[...] = (cot_ref[...].astype(F32) * conv).astype(BF16)
+    value_grad_ref[...] = grad_ref[...].astype(BF16)
     filt_ref[...] = x_ref[pl.ds(2 * width, rows, stride=stride), :].T.astype(BF16)
 
 
@@ -207,35 +215,42 @@
     parts = filters // blocks
     width = group * parts
     w1h, w1l, m2h, m2l, b1h, b1l, n2h, n2l, tc, ts = make_tables(rows, blocks)
-    gate = gate.reshape(rows, group * filters)
-    value = value.reshape(rows, group * filters)
-    cotangent = cotangent.reshape(rows, group * filters)
+    pair = np.concatenate([w1h, w1l], axis=1)
+    forward, backward, turns = (pair, w1h, m2h, m2l), (b1h, b1l, n2h, n2l), (tc, ts)
+
+    def to_rows(x):
+        x = x.reshape(rows, group, parts, blocks).transpose(0, 2, 1, 3)
+        return x.reshape(rows * width, blocks)
+
+    def from_rows(x):
+        x = x.reshape(rows, parts, group, blocks).transpose(0, 2, 1, 3)
+        return x.reshape(rows, group, filters)
 
     def shape(*dims, dtype=F32):
         return jax.ShapeDtypeStruct(dims, dtype)
 
+    gate, value, cotangent = to_rows(gate), to_rows(value), to_rows(cotangent)
+    wide = pltpu.VMEM((rows * width, blocks), F32)
     sent = call(
-        lambda *refs: pack_kernel(group, parts, *refs),
+        lambda *refs: pack_kernel(width, parts, *refs),
         shape(blocks * (2 * width + parts), rows),
         gate, value, cotangent, filt,
+        scratch_shapes=[wide, wide],
     )
     held = exchange(sent, blocks)
     scale = 1.0 / math.sqrt(rows * blocks)
-    hs, vs, gs, dh = call(
+    spectra = pltpu.VMEM((width * blocks, 2 * rows), F32)
+    dh = call(
         lambda *refs: spectra_kernel(group, parts, scale, *refs),
-        (
-            shape(parts * blocks, 2 * rows),
-            shape(width * blocks, 2 * rows),
-            shape(width * blocks, 2 * rows),
-            shape(parts, blocks, rows),
-        ),
-        held, w1h, w1l, m2h, m2l, b1h, b1l, n2h, n2l, tc, ts,
+        shape(parts, blocks, rows),
+        held, *forward, *backward, *turns,
+        scratch_shapes=[spectra, spectra],
     )
     dh = lax.all_to_all(dh, "ch", split_axis=0, concat_axis=0, tiled=True)
     big = call(
         lambda *refs: products_kernel(group, parts, *refs),
         shape(blocks * (2 * width + 1), rows),
-        hs, vs, gs, b1h, b1l, n2h, n2l, tc, ts,
+        held, *forward, *backward, *turns,
     )
     big = call(
         merge_kernel,
@@ -243,14 +258,14 @@
         dh, big,
     )
     back = exchange(big, blocks)
-    token = shape(rows, group * filters, dtype=BF16)
+    token = shape(rows * width, blocks, dtype=BF16)
     out, gate_grad, value_grad, filt_grad = call(
-        lambda *refs: unpack_kernel(group, parts, *refs),
+        lambda *refs: unpack_kernel(width, *refs),
         (token, token, token, shape(rows, blocks, dtype=BF16)),
         back, gate, cotangent,
-    )
-    full = (rows, group, filters)
-    return out.reshape(full), gate_grad.reshape(full), value_grad.reshape(full), filt_grad
+        scratch_shapes=[wide, wide],
+    )
+    return from_rows(out), from_rows(gate_grad), from_rows(value_grad), filt_grad
 
 
 def solution(mesh):

time: 117 us -> 115 us (0.983)
  local copies, waits for them, and re-layouts: 8.81 us -> 5.51 us
  Pallas kernels: 7.68 us -> 9.48 us
    reshape x3 -> x0, local copies, waits for them, and re-layouts: 2.64 us -> none  [the longest x1 0.88 us: per_device(): out.reshape(full)]
    pallas_call x5, Pallas kernels: 7.68 us -> 9.48 us  [call(): pl.pallas_call(body, out_shape=outs, in_specs=[VMEM] * len(args), out_spe...]
    unnamed x35 -> x36, local copies, waits for them, and re-layouts: 6.17 us -> 5.51 us
  transfers between devices with their start and end apart: 1 -> 1, of which waited for: 1 -> 0; matrix products, arithmetic and copies ran while one was open for 0% -> 0% of each run, Pallas kernels for 2% -> 4%
where the time goes in v1:
time: 115 us; the launch traced here: 114 us
  blocking collectives  94.4 us (82%)
  Pallas kernels  9.48 us (8%)
  local copies, waits for them, and re-layouts  5.51 us (5%)
  starting transfers between devices  4.02 us (3%)
    all_to_all x2, blocking collectives, exchange(): lax.all_to_all(flat, 'seq', split_axis=0, concat_axis=0, tiled=True)  94.4 us
    pallas_call x5, Pallas kernels, call(): pl.pallas_call(body, out_shape=outs, in_specs=[VMEM] * len(args), out_spe...  9.48 us
    unnamed x36, local copies, waits for them, and re-layouts  5.51 us
    all_to_all x1, starting transfers between devices, per_device(): dh = lax.all_to_all(dh, 'ch', split_axis=0, concat_axis=0, tiled=True)  4.02 us
  transfers between devices with their start and end apart: 1, of which 0 were waited for; matrix products, arithmetic and copies ran while one was open for 0% of the time, Pallas kernels for 4%

profile of v1, /device:TPU:1, one launch (start us, length us, event | category | flops | bytes accessed | tf_op | source)
XLA Modules:
  0.0 114.2 jit_solution(10159822033866523809)
XLA Ops:
  0.6 0.9 copy-done
  1.6 0.9 copy-done.2
  2.5 0.9 copy-done.9
  3.5 0.9 copy-done.17
  4.4 0.5 shard_map.165
  4.9 0.0 copy-start.4
  4.9 0.0 copy-start.5
  4.9 0.0 copy-start.6
  4.9 0.0 copy-start.7
  4.9 0.0 copy-start.8
  4.9 0.0 copy-start.10
  5.0 0.0 copy-start.11
  5.0 0.0 copy-start.12
  5.0 0.0 copy-start.13
  5.0 0.0 copy-start.15
  5.0 54.4 %all_to_all.23 = f32[128,1,2560]{2,1,0:T(1,128)S(1)} all-to-all(f32[128,1,2560]{2,1,0:T(1,128)S(1)} %bitcast.36), channel_id=1, replica_groups=mesh['seq'=128,'ch'=4] {'seq'}, dimensions={0} | all-to-all | bytes 2621440 | tf_op jit(solution)/shard_map/all_to_all | solution.py:209
  59.5 3.2 %shard_map.166 = f32[4,128,128]{2,1,0:T(8,128)} custom-call(f32[2560,128]{1,0:T(8,128)S(1)} %bitcast.34, bf16[256,256]{1,0:T(8,128)(2,1)S(1)} %copy-done.8, bf16[256,128]{1,0:T(8,128)(2,1)S(1)} %copy-done.15, bf16[256,256]{1,0:T(8,128)(2,1)S(1)} %copy-done.7, bf16[256,256]{1,0:T(8,128)(2,1)S(1)} %copy-done.6, bf16[128,256]{1,0:T(8,128)(2,1)S(1)} %copy-done.13, ...), custom_call_target="tpu_custom_call" | custom-call | tf_op jit(solution)/shard_map/pallas_call | solution.py:197
  62.7 4.0 %all-to-all-start.1 = ((f32[4,128,128]{2,1,0:T(8,128)}), f32[4,128,128]{2,1,0:T(8,128)S(1)}, u32[]{:S(2)}, u32[]{:S(2)}) async-start(f32[4,128,128]{2,1,0:T(8,128)} %shard_map.166), calls=%async_computation.1 | async-start | bytes 524288 | tf_op jit(solution)/shard_map/all_to_all | solution.py:249
  66.7 0.8 copy-done.14
  67.5 0.8 copy-done.16
  68.4 4.4 %shard_map.167.big_ref = f32[2176,128]{1,0:T(8,128)S(1)} custom-call(f32[2560,128]{1,0:T(8,128)S(1)} %bitcast.35, bf16[256,256]{1,0:T(8,128)(2,1)S(1)} %copy-done.8, bf16[256,128]{1,0:T(8,128)(2,1)S(1)} %copy-done.16, bf16[256,256]{1,0:T(8,128)(2,1)S(1)} %copy-done.7, bf16[256,256]{1,0:T(8,128)(2,1)S(1)} %copy-done.6, bf16[128,256]{1,0:T(8,128)(2,1)S(1)} %copy-done.14, ...), custom_call_target="tpu_custom_call" | custom-call | tf_op jit(solution)/shard_map/pallas_call | solution.py:197
  72.8 0.1 shard_map.168
  72.9 40.0 %all_to_all.24 = f32[128,1,2176]{2,1,0:T(1,128)S(1)} all-to-all(f32[128,1,2176]{2,1,0:T(1,128)S(1)} %bitcast.37), channel_id=1, replica_groups=mesh['seq'=128,'ch'=4] {'seq'}, dimensions={0} | all-to-all | bytes 2228224 | tf_op jit(solution)/shard_map/all_to_all | solution.py:209
  112.9 1.3 %shard_map.169 = (bf16[1024,128]{1,0:T(8,128)(2,1)}, bf16[1024,128]{1,0:T(8,128)(2,1)}, bf16[1024,128]{1,0:T(8,128)(2,1)}, bf16[128,128]{1,0:T(8,128)(2,1)}) custom-call(f32[2176,128]{1,0:T(8,128)S(1)} %bitcast.38, bf16[1024,128]{1,0:T(8,128)(2,1)S(1)} %bitcast.40, bf16[1024,128]{1,0:T(8,128)(2,1)S(1)} %bitcast.42), custom_call_target="tpu_custom_call" | custom-call | tf_op jit(solution)/shard_map/pallas_call | solution.py:197
  (21 shorter events, 0.0 us)
Async XLA Ops:
  0.6 1.0 copy-start
  1.6 0.9 copy-start.2
  2.5 0.9 copy-start.9
  3.5 0.9 copy-start.17
  4.9 54.5 %copy-start.4 = (bf16[256,256]{1,0:T(8,128)(2,1)S(1)}, bf16[256,256]{1,0:T(8,128)(2,1)}, u32[]{:S(2)}) copy-start(bf16[256,256]{1,0:T(8,128)(2,1)} %constant.27.clone.refs_8_) | copy-start | bytes 393220
  4.9 54.5 %copy-start.5 = (bf16[256,256]{1,0:T(8,128)(2,1)S(1)}, bf16[256,256]{1,0:T(8,128)(2,1)}, u32[]{:S(2)}) copy-start(bf16[256,256]{1,0:T(8,128)(2,1)} %constant.26.clone.refs_7_) | copy-start | bytes 393220
  4.9 54.5 %copy-start.6 = (bf16[256,256]{1,0:T(8,128)(2,1)S(1)}, bf16[256,256]{1,0:T(8,128)(2,1)}, u32[]{:S(2)}) copy-start(bf16[256,256]{1,0:T(8,128)(2,1)} %constant.23.clone.refs_4_) | copy-start | bytes 393220
  4.9 54.5 %copy-start.7 = (bf16[256,256]{1,0:T(8,128)(2,1)S(1)}, bf16[256,256]{1,0:T(8,128)(2,1)}, u32[]{:S(2)}) copy-start(bf16[256,256]{1,0:T(8,128)(2,1)} %constant.22.clone.refs_3_) | copy-start | bytes 393220
  4.9 54.5 %copy-start.8 = (bf16[256,256]{1,0:T(8,128)(2,1)S(1)}, bf16[256,256]{1,0:T(8,128)(2,1)}, u32[]{:S(2)}) copy-start(bf16[256,256]{1,0:T(8,128)(2,1)} %constant.20.clone.refs_1_) | copy-start | bytes 393220
  4.9 54.5 %copy-start.10 = (f32[128,128]{1,0:T(8,128)S(1)}, f32[128,128]{1,0:T(8,128)}, u32[]{:S(2)}) copy-start(f32[128,128]{1,0:T(8,128)} %constant.29.clone.refs_10_) | copy-start | bytes 196612
  5.0 54.5 %copy-start.11 = (f32[128,128]{1,0:T(8,128)S(1)}, f32[128,128]{1,0:T(8,128)}, u32[]{:S(2)}) copy-start(f32[128,128]{1,0:T(8,128)} %constant.28.clone.refs_9_) | copy-start | bytes 196612
  5.0 54.5 %copy-start.12 = (bf16[128,256]{1,0:T(8,128)(2,1)S(1)}, bf16[128,256]{1,0:T(8,128)(2,1)}, u32[]{:S(2)}) copy-start(bf16[128,256]{1,0:T(8,128)(2,1)} %constant.25.clone.refs_6_) | copy-start | bytes 196612
  5.0 54.5 %copy-start.13 = (bf16[128,256]{1,0:T(8,128)(2,1)S(1)}, bf16[128,256]{1,0:T(8,128)(2,1)}, u32[]{:S(2)}) copy-start(bf16[128,256]{1,0:T(8,128)(2,1)} %constant.24.clone.refs_5_) | copy-start | bytes 196612
  5.0 54.5 %copy-start.15 = (bf16[256,128]{1,0:T(8,128)(2,1)S(1)}, bf16[256,128]{1,0:T(8,128)(2,1)}, u32[]{:S(2)}) copy-start(bf16[256,128]{1,0:T(8,128)(2,1)} %constant.21.clone.refs_2_) | copy-start | bytes 196612
  62.7 10.1 %all-to-all-start.1 = ((f32[4,128,128]{2,1,0:T(8,128)}), f32[4,128,128]{2,1,0:T(8,128)S(1)}, u32[]{:S(2)}, u32[]{:S(2)}) async-start(f32[4,128,128]{2,1,0:T(8,128)} %shard_map.166), calls=%async_computation.1 | async-start | bytes 524288 | tf_op jit(solution)/shard_map/all_to_all | solution.py:249
  66.7 0.8 copy-start.14
  67.5 0.8 copy-start.16
  72.9 40.0 %copy-start.1 = (bf16[128,2,512]{2,1,0:T(2,128)(2,1)S(1)}, bf16[128,2,512]{2,1,0:T(2,128)(2,1)}, u32[]{:S(2)}) copy-start(bf16[128,2,512]{2,1,0:T(2,128)(2,1)} %param.14) | copy-start | bytes 786436
  72.9 40.0 %copy-start.3 = (bf16[128,2,512]{2,1,0:T(2,128)(2,1)S(1)}, bf16[128,2,512]{2,1,0:T(2,128)(2,1)}, u32[]{:S(2)}) copy-start(bf16[128,2,512]{2,1,0:T(2,128)(2,1)} %param.17) | copy-start | bytes 786436

commit v2 on v1

--- a/solution.py
+++ b/solution.py
@@ -11,7 +11,8 @@
 F32 = jnp.float32
 BF16 = jnp.bfloat16
 VMEM = pl.BlockSpec(memory_space=pltpu.VMEM)
-LIMIT = 24 * 1024 * 1024
+HBM = pl.BlockSpec(memory_space=pltpu.HBM)
+MIB = 1024 * 1024
 
 
 def two_parts(table):
@@ -35,10 +36,29 @@
     )
     back1 = stage1.T / (rows * blocks)
     back2 = stage2.T
-    parts = []
-    for table in (stage1, stage2, back1, back2):
-        parts.extend(two_parts(table))
-    return tuple(parts) + (np.cos(turn).astype(np.float32), np.sin(turn).astype(np.float32))
+    pieces = [np.concatenate(two_parts(stage1), axis=1)]
+    for table in (stage2, back2, back1):
+        pieces.extend(two_parts(table))
+    pieces.extend(two_parts(np.concatenate([np.cos(turn), np.sin(turn)], axis=1)))
+    return np.concatenate(pieces, axis=0)
+
+
+class Tables:
+    def __init__(self, table_ref):
+        full = table_ref.shape[1]
+        blocks = full // 2
+
+        def rows(first, count, lanes=full):
+            return table_ref[pl.ds(first, count), pl.ds(0, lanes)]
+
+        self.blocks = blocks
+        self.pair = lambda: rows(0, full)
+        self.stage1_high = lambda: rows(0, full, blocks)
+        self.stage2 = lambda: (rows(full, full), rows(2 * full, full))
+        self.back2 = lambda: (rows(3 * full, full), rows(4 * full, full))
+        self.back1 = lambda: (rows(5 * full, blocks), rows(5 * full + blocks, blocks))
+        turn = rows(6 * full, blocks).astype(F32) + rows(6 * full + blocks, blocks).astype(F32)
+        self.cos, self.sin = turn[:, :blocks], turn[:, blocks:]
 
 
 def split(x):
@@ -64,16 +84,16 @@
     return x[:, index * width:(index + 1) * width]
 
 
-def transform(x_ref, first, count, stride, exact, pair, high, m_high, m_low, tc, ts):
-    blocks = high.shape[1]
+def transform(x_ref, first, count, stride, exact, tables):
+    blocks, tc, ts = tables.blocks, tables.cos, tables.sin
     columns = [x_ref[pl.ds(first + c, blocks, stride=stride), :] for c in range(count)]
     x = jnp.concatenate(columns, axis=1)
     if exact:
         x = x.astype(BF16)
-        a = dot(pair[...], jnp.concatenate([x, x], axis=0))
+        a = dot(tables.pair(), jnp.concatenate([x, x], axis=0))
     else:
         x, low = split(x)
-        a = dot(pair[...], jnp.concatenate([x, x], axis=0)) + dot(high[...], low)
+        a = dot(tables.pair(), jnp.concatenate([x, x], axis=0)) + dot(tables.stage1_high(), low)
     re, im = a[:blocks], a[blocks:]
     pieces = []
     for c in range(count):
@@ -81,13 +101,13 @@
         pieces.append(
             jnp.concatenate([cr * tc + ci * ts, ci * tc - cr * ts], axis=1)
         )
-    return right_dot(jnp.concatenate(pieces, axis=0), m_high[...], m_low[...])
-
-
-def inverse(spectra, w_high, w_low, m_high, m_low, tc, ts):
-    blocks = w_high.shape[0]
+    return right_dot(jnp.concatenate(pieces, axis=0), *tables.stage2())
+
+
+def inverse(spectra, tables):
+    blocks, tc, ts = tables.blocks, tables.cos, tables.sin
     count = spectra.shape[0] // blocks
-    c = right_dot(spectra, m_high[...], m_low[...])
+    c = right_dot(spectra, *tables.back2())
     pieces = []
     for i in range(count):
         part = c[i * blocks:(i + 1) * blocks]
@@ -95,19 +115,30 @@
         pieces.append(
             jnp.concatenate([cr * tc - ci * ts, cr * ts + ci * tc], axis=0)
         )
-    return left_dot(w_high[...], w_low[...], jnp.concatenate(pieces, axis=1))
-
-
-def pack_kernel(width, parts, gate_ref, value_ref, cot_ref, filt_ref, out_ref, v_ref, g_ref):
+    return left_dot(*tables.back1(), jnp.concatenate(pieces, axis=1))
+
+
+def pack_kernel(
+    width, parts, gate_hbm, value_hbm, cot_hbm, filt_hbm, out_ref,
+    gate_ref, value_ref, cot_ref, filt_ref, v_ref, g_ref, sems,
+):
+    pairs = ((value_hbm, value_ref), (gate_hbm, gate_ref), (cot_hbm, cot_ref), (filt_hbm, filt_ref))
+    copies = [pltpu.make_async_copy(a, b, sems.at[i]) for i, (a, b) in enumerate(pairs)]
+    for copy in copies:
+        copy.start()
     rows = filt_ref.shape[0]
     stride = out_ref.shape[0] // rows
     scale = 1.0 / math.sqrt(rows * rows)
+    copies[0].wait()
     v_ref[...] = value_ref[...].astype(F32)
+    for c in range(width):
+        out_ref[pl.ds(c, rows, stride=stride), :] = v_ref[pl.ds(c, rows, stride=width), :].T
+    copies[1].wait()
+    copies[2].wait()
     g_ref[...] = cot_ref[...].astype(F32) * gate_ref[...].astype(F32)
     for c in range(width):
-        at = pl.ds(c, rows, stride=width)
-        out_ref[pl.ds(c, rows, stride=stride), :] = v_ref[at, :].T
-        out_ref[pl.ds(width + c, rows, stride=stride), :] = g_ref[at, :].T
+        out_ref[pl.ds(width + c, rows, stride=stride), :] = g_ref[pl.ds(c, rows, stride=width), :].T
+    copies[3].wait()
     for c in range(parts):
         out_ref[pl.ds(2 * width + c, rows, stride=stride), :] = (
             lanes(filt_ref, c).astype(F32) * scale
@@ -115,16 +146,14 @@
 
 
 def spectra_kernel(
-    group, parts, scale, x_ref, pair, w1h, m2h, m2l, b1h, b1l, n2h, n2l, tcr, tsr,
-    dh_ref, vs_ref, gs_ref,
+    group, parts, scale, x_ref, table_ref, dh_ref, vs_ref, gs_ref
 ):
-    blocks = w1h.shape[1]
+    tables = Tables(table_ref)
+    blocks = tables.blocks
     stride = x_ref.shape[0] // blocks
     width = group * parts
-    tc, ts = tcr[...], tsr[...]
-    fwd = (pair, w1h, m2h, m2l, tc, ts)
-    vs_ref[...] = transform(x_ref, 0, width, stride, True, *fwd)
-    gs_ref[...] = transform(x_ref, width, width, stride, False, *fwd)
+    vs_ref[...] = transform(x_ref, 0, width, stride, True, tables)
+    gs_ref[...] = transform(x_ref, width, width, stride, False, tables)
     pieces = []
     for q in range(parts):
         total_re = total_im = 0.0
@@ -135,24 +164,20 @@
             total_re += gr * vr + gi * vi
             total_im += gi * vr - gr * vi
         pieces.append(jnp.concatenate([total_re, total_im], axis=1))
-    dh = inverse(jnp.concatenate(pieces, axis=0), b1h, b1l, n2h, n2l, tc, ts)
+    dh = inverse(jnp.concatenate(pieces, axis=0), tables)
     for q in range(parts):
         dh_ref[q] = lanes(dh, q) * scale
 
 
-def products_kernel(
-    group, parts, x_ref, pair, w1h, m2h, m2l, b1h, b1l, n2h, n2l, tcr, tsr, out_ref
-):
-    blocks = w1h.shape[1]
+def products_kernel(group, parts, x_ref, table_ref, out_ref):
+    tables = Tables(table_ref)
+    blocks = tables.blocks
     stride = out_ref.shape[0] // blocks
     width = group * parts
-    tc, ts = tcr[...], tsr[...]
     held = x_ref.shape[0] // blocks
-    fwd = (pair, w1h, m2h, m2l, tc, ts)
-    inv = (b1h, b1l, n2h, n2l, tc, ts)
-    spectra = transform(x_ref, 2 * width, parts, held, True, *fwd)
+    spectra = transform(x_ref, 2 * width, parts, held, True, tables)
     for which in range(2):
-        signal = transform(x_ref, which * width, width, held, which == 0, *fwd)
+        signal = transform(x_ref, which * width, width, held, which == 0, tables)
         sign = 1.0 if which == 0 else -1.0
         pieces = []
         for c in range(width):
@@ -161,7 +186,7 @@
             h = spectra[q * blocks:(q + 1) * blocks]
             xr, xi, hr, hi = lanes(x, 0), lanes(x, 1), lanes(h, 0), lanes(h, 1) * sign
             pieces.append(jnp.concatenate([xr * hr - xi * hi, xr * hi + xi * hr], axis=1))
-        y = inverse(jnp.concatenate(pieces, axis=0), *inv)
+        y = inverse(jnp.concatenate(pieces, axis=0), tables)
         for c in range(width):
             out_ref[pl.ds(which * width + c, blocks, stride=stride), :] = lanes(y, c)
 
@@ -193,13 +218,13 @@
     filt_ref[...] = x_ref[pl.ds(2 * width, rows, stride=stride), :].T.astype(BF16)
 
 
-def call(body, outs, *args, **kw):
+def call(body, outs, *args, space=VMEM, limit=24 * MIB, **kw):
     return pl.pallas_call(
         body,
         out_shape=outs,
-        in_specs=[VMEM] * len(args),
+        in_specs=[space] * len(args),
         out_specs=jax.tree.map(lambda _: VMEM, outs),
-        compiler_params=pltpu.CompilerParams(vmem_limit_bytes=LIMIT),
+        compiler_params=pltpu.CompilerParams(vmem_limit_bytes=limit),
         **kw,
     )(*args)
 
@@ -214,9 +239,7 @@
     blocks = lax.axis_size("seq")
     parts = filters // blocks
     width = group * parts
-    w1h, w1l, m2h, m2l, b1h, b1l, n2h, n2l, tc, ts = make_tables(rows, blocks)
-    pair = np.concatenate([w1h, w1l], axis=1)
-    forward, backward, turns = (pair, w1h, m2h, m2l), (b1h, b1l, n2h, n2l), (tc, ts)
+    tables = make_tables(rows, blocks)
 
     def to_rows(x):
         x = x.reshape(rows, group, parts, blocks).transpose(0, 2, 1, 3)
@@ -235,7 +258,15 @@
         lambda *refs: pack_kernel(width, parts, *refs),
         shape(blocks * (2 * width + parts), rows),
         gate, value, cotangent, filt,
-        scratch_shapes=[wide, wide],
+        space=HBM,
+        limit=62 * MIB,
+        scratch_shapes=[
+            *[pltpu.VMEM((rows * width, blocks), BF16)] * 3,
+            pltpu.VMEM((rows, filters), BF16),
+            wide,
+            wide,
+            pltpu.SemaphoreType.DMA((4,)),
+        ],
     )
     held = exchange(sent, blocks)
     scale = 1.0 / math.sqrt(rows * blocks)
@@ -243,19 +274,20 @@
     dh = call(
         lambda *refs: spectra_kernel(group, parts, scale, *refs),
         shape(parts, blocks, rows),
-        held, *forward, *backward, *turns,
+        held, tables,
         scratch_shapes=[spectra, spectra],
     )
     dh = lax.all_to_all(dh, "ch", split_axis=0, concat_axis=0, tiled=True)
     big = call(
         lambda *refs: products_kernel(group, parts, *refs),
         shape(blocks * (2 * width + 1), rows),
-        held, *forward, *backward, *turns,
+        held, tables,
     )
     big = call(
         merge_kernel,
         shape(blocks * (2 * width + 1), rows),
         dh, big,
+        limit=6 * MIB,
     )
     back = exchange(big, blocks)
     token = shape(rows * width, blocks, dtype=BF16)
@@ -263,6 +295,7 @@
         lambda *refs: unpack_kernel(width, *refs),
         (token, token, token, shape(rows, blocks, dtype=BF16)),
         back, gate, cotangent,
+        limit=10 * MIB,
         scratch_shapes=[wide, wide],
     )
     return from_rows(out), from_rows(gate_grad), from_rows(value_grad), filt_grad

time: 115 us -> 114 us (level)
  local copies, waits for them, and re-layouts: 5.51 us -> 0.02 us
  Pallas kernels: 9.48 us -> 12.6 us
  waiting for transfers between devices: 0.01 us -> 1.45 us
    unnamed x36 -> x6, local copies, waits for them, and re-layouts: 5.51 us -> 0.02 us
    pallas_call x5, Pallas kernels: 9.48 us -> 12.6 us  [call(): pl.pallas_call(body, out_shape=outs, in_specs=[space] * len(args), out_sp...]
    all_to_all x1, waiting for transfers between devices: 0.01 us -> 1.45 us  [per_device(): dh = lax.all_to_all(dh, 'ch', split_axis=0, concat_axis=0, tiled=True)]
  transfers between devices with their start and end apart: 1 -> 1, of which waited for: 0 -> 1; matrix products, arithmetic and copies ran while one was open for 0% -> 0% of each run, Pallas kernels for 4% -> 4%
where the time goes in v2:
time: 114 us
  blocking collectives  94.9 us (83%)
  Pallas kernels  12.6 us (11%)
  starting transfers between devices  4.04 us (4%)
  waiting for transfers between devices  1.45 us (1%)
    all_to_all x2, blocking collectives, exchange(): lax.all_to_all(flat, 'seq', split_axis=0, concat_axis=0, tiled=True)  94.9 us
    pallas_call x5, Pallas kernels, call(): pl.pallas_call(body, out_shape=outs, in_specs=[space] * len(args), out_sp...  12.6 us
    all_to_all x1, starting transfers between devices, per_device(): dh = lax.all_to_all(dh, 'ch', split_axis=0, concat_axis=0, tiled=True)  4.04 us
  transfers between devices with their start and end apart: 1, of which 1 were waited for; matrix products, arithmetic and copies ran while one was open for 0% of the time, Pallas kernels for 4%

profile of v2, /device:TPU:1, one launch (start us, length us, event | category | flops | bytes accessed | tf_op | source)
XLA Modules:
  0.0 113.7 jit_solution(6444233160311315999)
XLA Ops:
  0.6 2.7 %shard_map.84 = f32[2560,128]{1,0:T(8,128)} custom-call(bf16[1024,128]{1,0:T(8,128)(2,1)} %bitcast.38, bf16[1024,128]{1,0:T(8,128)(2,1)} %bitcast.43, bf16[1024,128]{1,0:T(8,128)(2,1)} %bitcast.40, bf16[128,512]{1,0:T(8,128)(2,1)} %refs_3_.1), custom_call_target="tpu_custom_call" | custom-call | tf_op jit(solution)/shard_map/pallas_call | solution.py:222
  3.3 0.0 copy-start
  3.3 54.6 %all_to_all.23 = f32[128,1,2560]{2,1,0:T(1,128)S(1)} all-to-all(f32[128,1,2560]{2,1,0:T(1,128)} %bitcast.42), channel_id=1, replica_groups=mesh['seq'=128,'ch'=4] {'seq'}, dimensions={0} | all-to-all | bytes 2621440 | tf_op jit(solution)/shard_map/all_to_all | solution.py:234
  57.9 0.0 copy-done
  57.9 3.2 %shard_map.85 = f32[4,128,128]{2,1,0:T(8,128)} custom-call(f32[2560,128]{1,0:T(8,128)S(1)} %bitcast.34, bf16[1792,256]{1,0:T(8,128)(2,1)S(1)} %copy-done), custom_call_target="tpu_custom_call" | custom-call | tf_op jit(solution)/shard_map/pallas_call | solution.py:222
  61.1 4.0 %all-to-all-start.1 = ((f32[4,128,128]{2,1,0:T(8,128)}), f32[4,128,128]{2,1,0:T(8,128)}, u32[]{:S(2)}, u32[]{:S(2)}) async-start(f32[4,128,128]{2,1,0:T(8,128)} %shard_map.85), calls=%async_computation.1 | async-start | bytes 524288 | tf_op jit(solution)/shard_map/all_to_all | solution.py:280
  65.2 4.4 %shard_map.86.big_ref = f32[2176,128]{1,0:T(8,128)S(1)} custom-call(f32[2560,128]{1,0:T(8,128)S(1)} %bitcast.35, bf16[1792,256]{1,0:T(8,128)(2,1)S(1)} %copy-done), custom_call_target="tpu_custom_call" | custom-call | tf_op jit(solution)/shard_map/pallas_call | solution.py:222
  69.6 1.5 %all-to-all-done.1.dh_ref = f32[4,128,128]{2,1,0:T(8,128)} async-done(((f32[4,128,128]{2,1,0:T(8,128)}), f32[4,128,128]{2,1,0:T(8,128)}, u32[]{:S(2)}, u32[]{:S(2)}) %all-to-all-start.1) | async-done | bytes 262176 | tf_op jit(solution)/shard_map/all_to_all | solution.py:280
  71.0 1.0 shard_map.87
  72.0 0.0 copy-start.1
  72.1 0.0 copy-start.2
  72.1 40.3 %all_to_all.24 = f32[128,1,2176]{2,1,0:T(1,128)S(1)} all-to-all(f32[128,1,2176]{2,1,0:T(1,128)S(1)} %bitcast.36), channel_id=1, replica_groups=mesh['seq'=128,'ch'=4] {'seq'}, dimensions={0} | all-to-all | bytes 2228224 | tf_op jit(solution)/shard_map/all_to_all | solution.py:234
  112.4 0.0 copy-done.1
  112.4 0.0 copy-done.2
  112.4 1.3 %shard_map.88 = (bf16[1024,128]{1,0:T(8,128)(2,1)}, bf16[1024,128]{1,0:T(8,128)(2,1)}, bf16[1024,128]{1,0:T(8,128)(2,1)}, bf16[128,128]{1,0:T(8,128)(2,1)}) custom-call(f32[2176,128]{1,0:T(8,128)S(1)} %bitcast.37, bf16[1024,128]{1,0:T(8,128)(2,1)S(1)} %bitcast.39, bf16[1024,128]{1,0:T(8,128)(2,1)S(1)} %bitcast.41), custom_call_target="tpu_custom_call" | custom-call | tf_op jit(solution)/shard_map/pallas_call | solution.py:222
Async XLA Ops:
  3.3 54.6 %copy-start = (bf16[1792,256]{1,0:T(8,128)(2,1)S(1)}, bf16[1792,256]{1,0:T(8,128)(2,1)}, u32[]{:S(2)}) copy-start(bf16[1792,256]{1,0:T(8,128)(2,1)} %constant.2.clone.refs_1_) | copy-start | bytes 2752516
  61.1 9.9 %all-to-all-start.1 = ((f32[4,128,128]{2,1,0:T(8,128)}), f32[4,128,128]{2,1,0:T(8,128)}, u32[]{:S(2)}, u32[]{:S(2)}) async-start(f32[4,128,128]{2,1,0:T(8,128)} %shard_map.85), calls=%async_computation.1 | async-start | bytes 524288 | tf_op jit(solution)/shard_map/all_to_all | solution.py:280
  72.0 40.3 %copy-start.1 = (bf16[128,2,512]{2,1,0:T(2,128)(2,1)S(1)}, bf16[128,2,512]{2,1,0:T(2,128)(2,1)}, u32[]{:S(2)}) copy-start(bf16[128,2,512]{2,1,0:T(2,128)(2,1)} %param.5) | copy-start | bytes 786436
  72.1 40.3 %copy-start.2 = (bf16[128,2,512]{2,1,0:T(2,128)(2,1)S(1)}, bf16[128,2,512]{2,1,0:T(2,128)(2,1)}, u32[]{:S(2)}) copy-start(bf16[128,2,512]{2,1,0:T(2,128)(2,1)} %param.8) | copy-start | bytes 786436

commit v3 on v2

--- a/solution.py
+++ b/solution.py
@@ -13,6 +13,7 @@
 VMEM = pl.BlockSpec(memory_space=pltpu.VMEM)
 HBM = pl.BlockSpec(memory_space=pltpu.HBM)
 MIB = 1024 * 1024
+STRIDE = 19
 
 
 def two_parts(table):
@@ -21,7 +22,7 @@
     return high, low
 
 
-def make_tables(rows, blocks):
+def make_tables(rows, blocks, order):
     kappa = np.arange(blocks)[:, None]
     block = np.arange(blocks)[None, :]
     angle = math.pi / (2 * blocks) * ((2 * kappa + 1) * block % (4 * blocks))
@@ -34,6 +35,7 @@
     stage2 = np.concatenate(
         [np.concatenate([cos, -sin], axis=1), np.concatenate([sin, cos], axis=1)], axis=0
     )
+    stage1 = stage1[:, order]
     back1 = stage1.T / (rows * blocks)
     back2 = stage2.T
     pieces = [np.concatenate(two_parts(stage1), axis=1)]
@@ -229,9 +231,12 @@
     )(*args)
 
 
-def exchange(x, blocks):
-    flat = x.reshape(blocks, -1)
-    return lax.all_to_all(flat, "seq", split_axis=0, concat_axis=0, tiled=True).reshape(x.shape)
+def exchange(x, order):
+    flat = x.reshape(len(order), -1)
+    out = lax.all_to_all(
+        flat, "seq", split_axis=0, concat_axis=0, axis_index_groups=[order], tiled=True
+    )
+    return out.reshape(x.shape)
 
 
 def per_device(gate, value, filt, cotangent):
@@ -239,7 +244,8 @@
     blocks = lax.axis_size("seq")
     parts = filters // blocks
     width = group * parts
-    tables = make_tables(rows, blocks)
+    order = [STRIDE * i % blocks for i in range(blocks)]
+    tables = make_tables(rows, blocks, order)
 
     def to_rows(x):
         x = x.reshape(rows, group, parts, blocks).transpose(0, 2, 1, 3)
@@ -257,9 +263,9 @@
     sent = call(
         lambda *refs: pack_kernel(width, parts, *refs),
         shape(blocks * (2 * width + parts), rows),
-        gate, value, cotangent, filt,
+        *[pltpu.with_memory_space_constraint(x, pltpu.HBM) for x in (gate, value, cotangent, filt)],
         space=HBM,
-        limit=62 * MIB,
+        limit=24 * MIB,
         scratch_shapes=[
             *[pltpu.VMEM((rows * width, blocks), BF16)] * 3,
             pltpu.VMEM((rows, filters), BF16),
@@ -268,7 +274,7 @@
             pltpu.SemaphoreType.DMA((4,)),
         ],
     )
-    held = exchange(sent, blocks)
+    held = exchange(sent, order)
     scale = 1.0 / math.sqrt(rows * blocks)
     spectra = pltpu.VMEM((width * blocks, 2 * rows), F32)
     dh = call(
@@ -289,7 +295,7 @@
         dh, big,
         limit=6 * MIB,
     )
-    back = exchange(big, blocks)
+    back = exchange(big, order)
     token = shape(rows * width, blocks, dtype=BF16)
     out, gate_grad, value_grad, filt_grad = call(
         lambda *refs: unpack_kernel(width, *refs),

time: 114 us -> 114 us (level)
  no operation moved by 1% of the time
where the time goes in v3:
time: 114 us; the launch traced here: 113 us
  blocking collectives  96 us (84%)
  Pallas kernels  11.5 us (10%)
  starting transfers between devices  4.04 us (4%)
  waiting for transfers between devices  1.27 us (1%)
    all_to_all x2, blocking collectives, exchange(): lax.all_to_all(flat, 'seq', split_axis=0, concat_axis=0, axis_index_group...  96 us
    pallas_call x5, Pallas kernels, call(): pl.pallas_call(body, out_shape=outs, in_specs=[space] * len(args), out_sp...  11.5 us
    all_to_all x1, starting transfers between devices, per_device(): dh = lax.all_to_all(dh, 'ch', split_axis=0, concat_axis=0, tiled=True)  4.04 us
  transfers between devices with their start and end apart: 1, of which 1 were waited for; matrix products, arithmetic and copies ran while one was open for 0% of the time, Pallas kernels for 4%

profile of v3, /device:TPU:1, one launch (start us, length us, event | category | flops | bytes accessed | tf_op | source)
XLA Modules:
  0.0 113.5 jit_solution(3398160783715781986)
XLA Ops:
  0.6 1.6 %shard_map.84 = f32[2560,128]{1,0:T(8,128)S(1)} custom-call(bf16[1024,128]{1,0:T(8,128)(2,1)} %bitcast.39, bf16[1024,128]{1,0:T(8,128)(2,1)} %bitcast.43, bf16[1024,128]{1,0:T(8,128)(2,1)} %bitcast.41, bf16[128,512]{1,0:T(8,128)(2,1)} %refs_3_.1), custom_call_target="tpu_custom_call" | custom-call | tf_op jit(solution)/shard_map/pallas_call | solution.py:224
  2.2 0.0 copy-start
  2.3 55.5 %all_to_all.23 = f32[128,1,2560]{2,1,0:T(1,128)S(1)} all-to-all(f32[128,1,2560]{2,1,0:T(1,128)S(1)} %bitcast.36), channel_id=1, replica_groups={{0,76,152,228,304,380,456,20,96,172,248,324,400,476,40,116,192,268,344,..., dimensions={0} | all-to-all | bytes 2621440 | tf_op jit(solution)/shard_map/all_to_all | solution.py:236
  57.7 0.0 copy-done
  57.7 3.2 %shard_map.85 = f32[4,128,128]{2,1,0:T(8,128)} custom-call(f32[2560,128]{1,0:T(8,128)S(1)} %bitcast.34, bf16[1792,256]{1,0:T(8,128)(2,1)S(1)} %copy-done), custom_call_target="tpu_custom_call" | custom-call | tf_op jit(solution)/shard_map/pallas_call | solution.py:224
  60.9 4.0 %all-to-all-start.1 = ((f32[4,128,128]{2,1,0:T(8,128)}), f32[4,128,128]{2,1,0:T(8,128)}, u32[]{:S(2)}, u32[]{:S(2)}) async-start(f32[4,128,128]{2,1,0:T(8,128)} %shard_map.85), calls=%async_computation.1 | async-start | bytes 524288 | tf_op jit(solution)/shard_map/all_to_all | solution.py:286
  64.9 4.4 %shard_map.86.big_ref = f32[2176,128]{1,0:T(8,128)S(1)} custom-call(f32[2560,128]{1,0:T(8,128)S(1)} %bitcast.35, bf16[1792,256]{1,0:T(8,128)(2,1)S(1)} %copy-done), custom_call_target="tpu_custom_call" | custom-call | tf_op jit(solution)/shard_map/pallas_call | solution.py:224
  69.3 1.3 %all-to-all-done.1.dh_ref = f32[4,128,128]{2,1,0:T(8,128)} async-done(((f32[4,128,128]{2,1,0:T(8,128)}), f32[4,128,128]{2,1,0:T(8,128)}, u32[]{:S(2)}, u32[]{:S(2)}) %all-to-all-start.1) | async-done | bytes 262176 | tf_op jit(solution)/shard_map/all_to_all | solution.py:286
  70.6 1.0 shard_map.87
  71.6 0.0 copy-start.1
  71.6 0.0 copy-start.2
  71.7 40.5 %all_to_all.24 = f32[128,1,2176]{2,1,0:T(1,128)S(1)} all-to-all(f32[128,1,2176]{2,1,0:T(1,128)S(1)} %bitcast.37), channel_id=1, replica_groups={{0,76,152,228,304,380,456,20,96,172,248,324,400,476,40,116,192,268,344,..., dimensions={0} | all-to-all | bytes 2228224 | tf_op jit(solution)/shard_map/all_to_all | solution.py:236
  112.2 0.0 copy-done.1
  112.2 0.0 copy-done.2
  112.2 1.3 %shard_map.88 = (bf16[1024,128]{1,0:T(8,128)(2,1)}, bf16[1024,128]{1,0:T(8,128)(2,1)}, bf16[1024,128]{1,0:T(8,128)(2,1)}, bf16[128,128]{1,0:T(8,128)(2,1)}) custom-call(f32[2176,128]{1,0:T(8,128)S(1)} %bitcast.38, bf16[1024,128]{1,0:T(8,128)(2,1)S(1)} %bitcast.40, bf16[1024,128]{1,0:T(8,128)(2,1)S(1)} %bitcast.42), custom_call_target="tpu_custom_call" | custom-call | tf_op jit(solution)/shard_map/pallas_call | solution.py:224
Async XLA Ops:
  2.2 55.5 %copy-start = (bf16[1792,256]{1,0:T(8,128)(2,1)S(1)}, bf16[1792,256]{1,0:T(8,128)(2,1)}, u32[]{:S(2)}) copy-start(bf16[1792,256]{1,0:T(8,128)(2,1)} %constant.2.clone.refs_1_) | copy-start | bytes 2752516
  60.9 9.7 %all-to-all-start.1 = ((f32[4,128,128]{2,1,0:T(8,128)}), f32[4,128,128]{2,1,0:T(8,128)}, u32[]{:S(2)}, u32[]{:S(2)}) async-start(f32[4,128,128]{2,1,0:T(8,128)} %shard_map.85), calls=%async_computation.1 | async-start | bytes 524288 | tf_op jit(solution)/shard_map/all_to_all | solution.py:286
  71.6 40.5 %copy-start.1 = (bf16[128,2,512]{2,1,0:T(2,128)(2,1)S(1)}, bf16[128,2,512]{2,1,0:T(2,128)(2,1)}, u32[]{:S(2)}) copy-start(bf16[128,2,512]{2,1,0:T(2,128)(2,1)} %param.5) | copy-start | bytes 786436
  71.6 40.5 %copy-start.2 = (bf16[128,2,512]{2,1,0:T(2,128)(2,1)S(1)}, bf16[128,2,512]{2,1,0:T(2,128)(2,1)}, u32[]{:S(2)}) copy-start(bf16[128,2,512]{2,1,0:T(2,128)(2,1)} %param.8) | copy-start | bytes 786436

commit v4 on v3

--- a/solution.py
+++ b/solution.py
@@ -86,9 +86,10 @@
     return x[:, index * width:(index + 1) * width]
 
 
-def transform(x_ref, first, count, stride, exact, tables):
+def transform(x_ref, firsts, stride, exact, tables):
     blocks, tc, ts = tables.blocks, tables.cos, tables.sin
-    columns = [x_ref[pl.ds(first + c, blocks, stride=stride), :] for c in range(count)]
+    count = len(firsts)
+    columns = [x_ref[pl.ds(first, blocks, stride=stride), :] for first in firsts]
     x = jnp.concatenate(columns, axis=1)
     if exact:
         x = x.astype(BF16)
@@ -147,43 +148,50 @@
         ).T
 
 
-def spectra_kernel(
-    group, parts, scale, x_ref, table_ref, dh_ref, vs_ref, gs_ref
-):
+def correlation(vs_ref, gs_ref, firsts, blocks):
+    total_re = total_im = 0.0
+    for first in firsts:
+        v, g = vs_ref[pl.ds(first, blocks), :], gs_ref[pl.ds(first, blocks), :]
+        vr, vi, gr, gi = lanes(v, 0), lanes(v, 1), lanes(g, 0), lanes(g, 1)
+        total_re += gr * vr + gi * vi
+        total_im += gi * vr - gr * vi
+    return jnp.concatenate([total_re, total_im], axis=1)
+
+
+def others_kernel(group, parts, scale, x_ref, table_ref, dh_ref, vs_ref, gs_ref):
     tables = Tables(table_ref)
     blocks = tables.blocks
     stride = x_ref.shape[0] // blocks
     width = group * parts
-    vs_ref[...] = transform(x_ref, 0, width, stride, True, tables)
-    gs_ref[...] = transform(x_ref, width, width, stride, False, tables)
-    pieces = []
-    for q in range(parts):
-        total_re = total_im = 0.0
-        for s in range(group):
-            at = pl.ds((q * group + s) * blocks, blocks)
-            v, g = vs_ref[at, :], gs_ref[at, :]
-            vr, vi, gr, gi = lanes(v, 0), lanes(v, 1), lanes(g, 0), lanes(g, 1)
-            total_re += gr * vr + gi * vi
-            total_im += gi * vr - gr * vi
-        pieces.append(jnp.concatenate([total_re, total_im], axis=1))
+    me = lax.axis_index("ch")
+    others = [lax.rem(me + k, parts) for k in range(1, parts)]
+    columns = [q * group + s for q in others for s in range(group)]
+    vs_ref[...] = transform(x_ref, columns, stride, True, tables)
+    gs_ref[...] = transform(x_ref, [width + c for c in columns], stride, False, tables)
+    pieces = [
+        correlation(vs_ref, gs_ref, [(i * group + s) * blocks for s in range(group)], blocks)
+        for i in range(parts - 1)
+    ]
     dh = inverse(jnp.concatenate(pieces, axis=0), tables)
-    for q in range(parts):
-        dh_ref[q] = lanes(dh, q) * scale
-
-
-def products_kernel(group, parts, x_ref, table_ref, out_ref):
+    for i, q in enumerate(others):
+        dh_ref[q] = lanes(dh, i) * scale
+    dh_ref[me] = jnp.zeros_like(dh_ref[me])
+
+
+def products_kernel(group, parts, scale, x_ref, table_ref, out_ref, vs_ref, gs_ref):
     tables = Tables(table_ref)
     blocks = tables.blocks
     stride = out_ref.shape[0] // blocks
     width = group * parts
     held = x_ref.shape[0] // blocks
-    spectra = transform(x_ref, 2 * width, parts, held, True, tables)
-    for which in range(2):
-        signal = transform(x_ref, which * width, width, held, which == 0, tables)
+    spectra = transform(x_ref, [2 * width + q for q in range(parts)], held, True, tables)
+    for which, ref in enumerate((vs_ref, gs_ref)):
+        columns = [which * width + c for c in range(width)]
+        ref[...] = transform(x_ref, columns, held, which == 0, tables)
         sign = 1.0 if which == 0 else -1.0
         pieces = []
         for c in range(width):
-            x = signal[c * blocks:(c + 1) * blocks]
+            x = ref[pl.ds(c * blocks, blocks), :]
             q = c // group
             h = spectra[q * blocks:(q + 1) * blocks]
             xr, xi, hr, hi = lanes(x, 0), lanes(x, 1), lanes(h, 0), lanes(h, 1) * sign
@@ -191,44 +199,70 @@
         y = inverse(jnp.concatenate(pieces, axis=0), tables)
         for c in range(width):
             out_ref[pl.ds(which * width + c, blocks, stride=stride), :] = lanes(y, c)
-
-
-def merge_kernel(dh_ref, big_ref, out_ref):
-    parts, blocks, rows = dh_ref.shape
+    me = lax.axis_index("ch")
+    own = [pl.multiple_of((me * group + s) * blocks, blocks) for s in range(group)]
+    dh = inverse(correlation(vs_ref, gs_ref, own, blocks), tables)
+    out_ref[pl.ds(2 * width, blocks, stride=stride), :] = dh * scale
+
+
+def merge_kernel(dh_hbm, big_ref, out_ref, dh_ref, sems):
+    parts, blocks, rows = dh_hbm.shape
+    copies = [pltpu.make_async_copy(dh_hbm.at[q], dh_ref.at[q], sems.at[q]) for q in range(parts)]
+    for copy in copies:
+        copy.start()
     stride = out_ref.shape[0] // blocks
     out_ref[...] = big_ref[...]
-    total = dh_ref[0]
-    for q in range(1, parts):
+    last = pl.ds(stride - 1, blocks, stride=stride)
+    total = big_ref[last, :]
+    for q in range(parts):
+        copies[q].wait()
         total += dh_ref[q]
-    out_ref[pl.ds(stride - 1, blocks, stride=stride), :] = total
+    out_ref[last, :] = total
 
 
 def unpack_kernel(
-    width, x_ref, gate_ref, cot_ref, out_ref, gate_grad_ref, value_grad_ref, filt_ref,
-    conv_ref, grad_ref,
+    width, x_ref, gate_ref, cot_ref, out_hbm, gate_grad_hbm, value_grad_hbm, filt_hbm,
+    conv_ref, grad_ref, out_ref, gate_grad_ref, value_grad_ref, filt_ref, sems,
 ):
+    pairs = (
+        (out_ref, out_hbm),
+        (gate_grad_ref, gate_grad_hbm),
+        (value_grad_ref, value_grad_hbm),
+        (filt_ref, filt_hbm),
+    )
+    copies = [pltpu.make_async_copy(a, b, sems.at[i]) for i, (a, b) in enumerate(pairs)]
     rows = filt_ref.shape[0]
     stride = x_ref.shape[0] // rows
     for c in range(width):
-        at = pl.ds(c, rows, stride=width)
-        conv_ref[at, :] = x_ref[pl.ds(c, rows, stride=stride), :].T
-        grad_ref[at, :] = x_ref[pl.ds(width + c, rows, stride=stride), :].T
+        conv_ref[pl.ds(c, rows, stride=width), :] = x_ref[pl.ds(c, rows, stride=stride), :].T
     conv = conv_ref[...]
     out_ref[...] = (gate_ref[...].astype(F32) * conv).astype(BF16)
+    copies[0].start()
     gate_grad_ref[...] = (cot_ref[...].astype(F32) * conv).astype(BF16)
+    copies[1].start()
+    for c in range(width):
+        grad_ref[pl.ds(c, rows, stride=width), :] = x_ref[pl.ds(width + c, rows, stride=stride), :].T
     value_grad_ref[...] = grad_ref[...].astype(BF16)
+    copies[2].start()
     filt_ref[...] = x_ref[pl.ds(2 * width, rows, stride=stride), :].T.astype(BF16)
-
-
-def call(body, outs, *args, space=VMEM, limit=24 * MIB, **kw):
+    copies[3].start()
+    for copy in copies:
+        copy.wait()
+
+
+def call(body, outs, *args, spaces=None, out_space=VMEM, limit=24 * MIB, **kw):
     return pl.pallas_call(
         body,
         out_shape=outs,
-        in_specs=[space] * len(args),
-        out_specs=jax.tree.map(lambda _: VMEM, outs),
+        in_specs=spaces or [VMEM] * len(args),
+        out_specs=jax.tree.map(lambda _: out_space, outs),
         compiler_params=pltpu.CompilerParams(vmem_limit_bytes=limit),
         **kw,
     )(*args)
+
+
+def in_hbm(x):
+    return pltpu.with_memory_space_constraint(x, pltpu.HBM)
 
 
 def exchange(x, order):
@@ -263,8 +297,8 @@
     sent = call(
         lambda *refs: pack_kernel(width, parts, *refs),
         shape(blocks * (2 * width + parts), rows),
-        *[pltpu.with_memory_space_constraint(x, pltpu.HBM) for x in (gate, value, cotangent, filt)],
-        space=HBM,
+        *[in_hbm(x) for x in (gate, value, cotangent, filt)],
+        spaces=[HBM] * 4,
         limit=24 * MIB,
         scratch_shapes=[
             *[pltpu.VMEM((rows * width, blocks), BF16)] * 3,
@@ -276,24 +310,31 @@
     )
     held = exchange(sent, order)
     scale = 1.0 / math.sqrt(rows * blocks)
-    spectra = pltpu.VMEM((width * blocks, 2 * rows), F32)
+    some = pltpu.VMEM(((parts - 1) * group * blocks, 2 * rows), F32)
     dh = call(
-        lambda *refs: spectra_kernel(group, parts, scale, *refs),
+        lambda *refs: others_kernel(group, parts, scale, *refs),
         shape(parts, blocks, rows),
         held, tables,
-        scratch_shapes=[spectra, spectra],
+        scratch_shapes=[some, some],
     )
     dh = lax.all_to_all(dh, "ch", split_axis=0, concat_axis=0, tiled=True)
+    spectra = pltpu.VMEM((width * blocks, 2 * rows), F32)
     big = call(
-        lambda *refs: products_kernel(group, parts, *refs),
+        lambda *refs: products_kernel(group, parts, scale, *refs),
         shape(blocks * (2 * width + 1), rows),
         held, tables,
+        scratch_shapes=[spectra, spectra],
     )
     big = call(
         merge_kernel,
         shape(blocks * (2 * width + 1), rows),
-        dh, big,
+        in_hbm(dh), big,
+        spaces=[HBM, VMEM],
         limit=6 * MIB,
+        scratch_shapes=[
+            pltpu.VMEM((parts, blocks, rows), F32),
+            pltpu.SemaphoreType.DMA((parts,)),
+        ],
     )
     back = exchange(big, order)
     token = shape(rows * width, blocks, dtype=BF16)
@@ -301,8 +342,15 @@
         lambda *refs: unpack_kernel(width, *refs),
         (token, token, token, shape(rows, blocks, dtype=BF16)),
         back, gate, cotangent,
+        out_space=HBM,
         limit=10 * MIB,
-        scratch_shapes=[wide, wide],
+        scratch_shapes=[
+            wide,
+            wide,
+            *[pltpu.VMEM((rows * width, blocks), BF16)] * 3,
+            pltpu.VMEM((rows, blocks), BF16),
+            pltpu.SemaphoreType.DMA((4,)),
+        ],
     )
     return from_rows(out), from_rows(gate_grad), from_rows(value_grad), filt_grad
 

time: 114 us -> 113 us (level)
  no operation moved by 1% of the time
where the time goes in v4:
time: 113 us
  blocking collectives  96 us (85%)
  Pallas kernels  10.9 us (10%)
  starting transfers between devices  4.04 us (4%)
  waiting for transfers between devices  1.16 us (1%)
    all_to_all x2, blocking collectives, exchange(): lax.all_to_all(flat, 'seq', split_axis=0, concat_axis=0, axis_index_group...  96 us
    pallas_call x5, Pallas kernels, call(): pl.pallas_call(body, out_shape=outs, in_specs=spaces or [VMEM] * len(args...  10.9 us
    all_to_all x1, starting transfers between devices, per_device(): dh = lax.all_to_all(dh, 'ch', split_axis=0, concat_axis=0, tiled=True)  4.04 us
  transfers between devices with their start and end apart: 1, of which 1 were waited for; matrix products, arithmetic and copies ran while one was open for 0% of the time, Pallas kernels for 4%

profile of v4, /device:TPU:1, one launch (start us, length us, event | category | flops | bytes accessed | tf_op | source)
XLA Modules:
  0.0 112.8 jit_solution(9329780606642263456)
XLA Ops:
  0.6 1.6 %shard_map.84 = f32[2560,128]{1,0:T(8,128)S(1)} custom-call(bf16[1024,128]{1,0:T(8,128)(2,1)} %bitcast.39, bf16[1024,128]{1,0:T(8,128)(2,1)} %bitcast.43, bf16[1024,128]{1,0:T(8,128)(2,1)} %bitcast.41, bf16[128,512]{1,0:T(8,128)(2,1)} %refs_3_.1), custom_call_target="tpu_custom_call" | custom-call | tf_op jit(solution)/shard_map/pallas_call | solution.py:254
  2.2 0.0 copy-start
  2.3 55.5 %all_to_all.23 = f32[128,1,2560]{2,1,0:T(1,128)S(1)} all-to-all(f32[128,1,2560]{2,1,0:T(1,128)S(1)} %bitcast.36), channel_id=1, replica_groups={{0,76,152,228,304,380,456,20,96,172,248,324,400,476,40,116,192,268,344,..., dimensions={0} | all-to-all | bytes 2621440 | tf_op jit(solution)/shard_map/all_to_all | solution.py:270
  57.7 0.0 copy-done
  57.7 2.7 %shard_map.85 = f32[4,128,128]{2,1,0:T(8,128)} custom-call(f32[2560,128]{1,0:T(8,128)S(1)} %bitcast.34, bf16[1792,256]{1,0:T(8,128)(2,1)S(1)} %copy-done), custom_call_target="tpu_custom_call" | custom-call | tf_op jit(solution)/shard_map/pallas_call | solution.py:254
  60.4 4.0 %all-to-all-start.1 = ((f32[4,128,128]{2,1,0:T(8,128)}), f32[4,128,128]{2,1,0:T(8,128)}, u32[]{:S(2)}, u32[]{:S(2)}) async-start(f32[4,128,128]{2,1,0:T(8,128)} %shard_map.85), calls=%async_computation.1 | async-start | bytes 524288 | tf_op jit(solution)/shard_map/all_to_all | solution.py:320
  64.4 4.5 %shard_map.86.big_ref = f32[2176,128]{1,0:T(8,128)S(1)} custom-call(f32[2560,128]{1,0:T(8,128)S(1)} %bitcast.35, bf16[1792,256]{1,0:T(8,128)(2,1)S(1)} %copy-done), custom_call_target="tpu_custom_call" | custom-call | tf_op jit(solution)/shard_map/pallas_call | solution.py:254
  68.9 1.2 %all-to-all-done.1.dh_hbm = f32[4,128,128]{2,1,0:T(8,128)} async-done(((f32[4,128,128]{2,1,0:T(8,128)}), f32[4,128,128]{2,1,0:T(8,128)}, u32[]{:S(2)}, u32[]{:S(2)}) %all-to-all-start.1) | async-done | bytes 262176 | tf_op jit(solution)/shard_map/all_to_all | solution.py:320
  70.1 1.0 shard_map.87
  71.1 0.0 copy-start.1
  71.1 0.0 copy-start.2
  71.1 40.5 %all_to_all.24 = f32[128,1,2176]{2,1,0:T(1,128)S(1)} all-to-all(f32[128,1,2176]{2,1,0:T(1,128)S(1)} %bitcast.37), channel_id=1, replica_groups={{0,76,152,228,304,380,456,20,96,172,248,324,400,476,40,116,192,268,344,..., dimensions={0} | all-to-all | bytes 2228224 | tf_op jit(solution)/shard_map/all_to_all | solution.py:270
  111.6 0.0 copy-done.1
  111.6 0.0 copy-done.2
  111.6 1.2 %shard_map.88 = (bf16[1024,128]{1,0:T(8,128)(2,1)}, bf16[1024,128]{1,0:T(8,128)(2,1)}, bf16[1024,128]{1,0:T(8,128)(2,1)}, bf16[128,128]{1,0:T(8,128)(2,1)}) custom-call(f32[2176,128]{1,0:T(8,128)S(1)} %bitcast.38, bf16[1024,128]{1,0:T(8,128)(2,1)S(1)} %bitcast.40, bf16[1024,128]{1,0:T(8,128)(2,1)S(1)} %bitcast.42), custom_call_target="tpu_custom_call" | custom-call | tf_op jit(solution)/shard_map/pallas_call | solution.py:254
Async XLA Ops:
  2.2 55.5 %copy-start = (bf16[1792,256]{1,0:T(8,128)(2,1)S(1)}, bf16[1792,256]{1,0:T(8,128)(2,1)}, u32[]{:S(2)}) copy-start(bf16[1792,256]{1,0:T(8,128)(2,1)} %constant.2.clone.refs_1_) | copy-start | bytes 2752516
  60.4 9.7 %all-to-all-start.1 = ((f32[4,128,128]{2,1,0:T(8,128)}), f32[4,128,128]{2,1,0:T(8,128)}, u32[]{:S(2)}, u32[]{:S(2)}) async-start(f32[4,128,128]{2,1,0:T(8,128)} %shard_map.85), calls=%async_computation.1 | async-start | bytes 524288 | tf_op jit(solution)/shard_map/all_to_all | solution.py:320
  71.1 40.5 %copy-start.1 = (bf16[128,2,512]{2,1,0:T(2,128)(2,1)S(1)}, bf16[128,2,512]{2,1,0:T(2,128)(2,1)}, u32[]{:S(2)}) copy-start(bf16[128,2,512]{2,1,0:T(2,128)(2,1)} %param.5) | copy-start | bytes 786436
  71.1 40.5 %copy-start.2 = (bf16[128,2,512]{2,1,0:T(2,128)(2,1)S(1)}, bf16[128,2,512]{2,1,0:T(2,128)(2,1)}, u32[]{:S(2)}) copy-start(bf16[128,2,512]{2,1,0:T(2,128)(2,1)} %param.8) | copy-start | bytes 786436

commit v5 on v4

--- a/solution.py
+++ b/solution.py
@@ -14,6 +14,7 @@
 HBM = pl.BlockSpec(memory_space=pltpu.HBM)
 MIB = 1024 * 1024
 STRIDE = 19
+LATE = 1
 
 
 def two_parts(table):
@@ -74,12 +75,14 @@
 
 def left_dot(high, low, x):
     x_high, x_low = split(x)
-    return dot(high, x_high) + dot(high, x_low) + dot(low, x_high)
+    table = jnp.concatenate([high, high, low], axis=1)
+    return dot(table, jnp.concatenate([x_high, x_low, x_high], axis=0))
 
 
 def right_dot(x, high, low):
     x_high, x_low = split(x)
-    return dot(x_high, high) + dot(x_low, high) + dot(x_high, low)
+    table = jnp.concatenate([high, high, low], axis=0)
+    return dot(jnp.concatenate([x_high, x_low, x_high], axis=1), table)
 
 
 def lanes(x, index, width=128):
@@ -181,8 +184,9 @@
 def products_kernel(group, parts, scale, x_ref, table_ref, out_ref, vs_ref, gs_ref):
     tables = Tables(table_ref)
     blocks = tables.blocks
-    stride = out_ref.shape[0] // blocks
     width = group * parts
+    stride = 2 * width + 1
+    late = (out_ref.shape[0] // blocks - stride) // 2
     held = x_ref.shape[0] // blocks
     spectra = transform(x_ref, [2 * width + q for q in range(parts)], held, True, tables)
     for which, ref in enumerate((vs_ref, gs_ref)):
@@ -196,22 +200,35 @@
             h = spectra[q * blocks:(q + 1) * blocks]
             xr, xi, hr, hi = lanes(x, 0), lanes(x, 1), lanes(h, 0), lanes(h, 1) * sign
             pieces.append(jnp.concatenate([xr * hr - xi * hi, xr * hi + xi * hr], axis=1))
-        y = inverse(jnp.concatenate(pieces, axis=0), tables)
-        for c in range(width):
+        here = width if which == 0 else width - late
+        y = inverse(jnp.concatenate(pieces[:here], axis=0), tables)
+        for c in range(here):
             out_ref[pl.ds(which * width + c, blocks, stride=stride), :] = lanes(y, c)
+        if here < width:
+            rest = jnp.concatenate(pieces[here:], axis=0)
+            for half in range(2):
+                at = pl.ds((stride + half * late) * blocks, late * blocks)
+                out_ref[at, :] = lanes(rest, half)
     me = lax.axis_index("ch")
     own = [pl.multiple_of((me * group + s) * blocks, blocks) for s in range(group)]
     dh = inverse(correlation(vs_ref, gs_ref, own, blocks), tables)
     out_ref[pl.ds(2 * width, blocks, stride=stride), :] = dh * scale
 
 
-def merge_kernel(dh_hbm, big_ref, out_ref, dh_ref, sems):
+def merge_kernel(dh_hbm, big_ref, table_ref, out_ref, dh_ref, sems):
     parts, blocks, rows = dh_hbm.shape
     copies = [pltpu.make_async_copy(dh_hbm.at[q], dh_ref.at[q], sems.at[q]) for q in range(parts)]
     for copy in copies:
         copy.start()
     stride = out_ref.shape[0] // blocks
-    out_ref[...] = big_ref[...]
+    out_ref[...] = big_ref[pl.ds(0, stride * blocks), :]
+    late = (big_ref.shape[0] // blocks - stride) // 2
+    rest = [
+        big_ref[pl.ds((stride + half * late) * blocks, late * blocks), :] for half in range(2)
+    ]
+    y = inverse(jnp.concatenate(rest, axis=1), Tables(table_ref))
+    for c in range(late):
+        out_ref[pl.ds(stride - 1 - late + c, blocks, stride=stride), :] = lanes(y, c)
     last = pl.ds(stride - 1, blocks, stride=stride)
     total = big_ref[last, :]
     for q in range(parts):
@@ -321,16 +338,16 @@
     spectra = pltpu.VMEM((width * blocks, 2 * rows), F32)
     big = call(
         lambda *refs: products_kernel(group, parts, scale, *refs),
-        shape(blocks * (2 * width + 1), rows),
+        shape(blocks * (2 * width + 1 + 2 * LATE), rows),
         held, tables,
         scratch_shapes=[spectra, spectra],
     )
     big = call(
         merge_kernel,
         shape(blocks * (2 * width + 1), rows),
-        in_hbm(dh), big,
-        spaces=[HBM, VMEM],
-        limit=6 * MIB,
+        in_hbm(dh), big, tables,
+        spaces=[HBM, VMEM, VMEM],
+        limit=12 * MIB,
         scratch_shapes=[
             pltpu.VMEM((parts, blocks, rows), F32),
             pltpu.SemaphoreType.DMA((parts,)),

time: 113 us -> 113 us (level)
  no operation moved by 1% of the time
where the time goes in v5:
time: 113 us
  blocking collectives  96 us (85%)
  Pallas kernels  11 us (10%)
  starting transfers between devices  4.04 us (4%)
  waiting for transfers between devices  1.14 us (1%)
    all_to_all x2, blocking collectives, exchange(): lax.all_to_all(flat, 'seq', split_axis=0, concat_axis=0, axis_index_group...  96 us
    pallas_call x5, Pallas kernels, call(): pl.pallas_call(body, out_shape=outs, in_specs=spaces or [VMEM] * len(args...  11 us
    all_to_all x1, starting transfers between devices, per_device(): dh = lax.all_to_all(dh, 'ch', split_axis=0, concat_axis=0, tiled=True)  4.04 us
  transfers between devices with their start and end apart: 1, of which 1 were waited for; matrix products, arithmetic and copies ran while one was open for 0% of the time, Pallas kernels for 4%

profile of v5, /device:TPU:1, one launch (start us, length us, event | category | flops | bytes accessed | tf_op | source)
XLA Modules:
  0.0 112.8 jit_solution(7073468739397678242)
XLA Ops:
  0.6 1.6 %shard_map.84 = f32[2560,128]{1,0:T(8,128)S(1)} custom-call(bf16[1024,128]{1,0:T(8,128)(2,1)} %bitcast.39, bf16[1024,128]{1,0:T(8,128)(2,1)} %bitcast.43, bf16[1024,128]{1,0:T(8,128)(2,1)} %bitcast.41, bf16[128,512]{1,0:T(8,128)(2,1)} %refs_3_.1), custom_call_target="tpu_custom_call" | custom-call | tf_op jit(solution)/shard_map/pallas_call | solution.py:271
  2.2 0.0 copy-start
  2.3 55.5 %all_to_all.23 = f32[128,1,2560]{2,1,0:T(1,128)S(1)} all-to-all(f32[128,1,2560]{2,1,0:T(1,128)S(1)} %bitcast.36), channel_id=1, replica_groups={{0,76,152,228,304,380,456,20,96,172,248,324,400,476,40,116,192,268,344,..., dimensions={0} | all-to-all | bytes 2621440 | tf_op jit(solution)/shard_map/all_to_all | solution.py:287
  57.7 0.0 copy-done
  57.7 2.7 %shard_map.85 = f32[4,128,128]{2,1,0:T(8,128)} custom-call(f32[2560,128]{1,0:T(8,128)S(1)} %bitcast.34, bf16[1792,256]{1,0:T(8,128)(2,1)S(1)} %copy-done), custom_call_target="tpu_custom_call" | custom-call | tf_op jit(solution)/shard_map/pallas_call | solution.py:271
  60.4 4.0 %all-to-all-start.1 = ((f32[4,128,128]{2,1,0:T(8,128)}), f32[4,128,128]{2,1,0:T(8,128)}, u32[]{:S(2)}, u32[]{:S(2)}) async-start(f32[4,128,128]{2,1,0:T(8,128)} %shard_map.85), calls=%async_computation.1 | async-start | bytes 524288 | tf_op jit(solution)/shard_map/all_to_all | solution.py:337
  64.4 4.5 %shard_map.86.big_ref = f32[2432,128]{1,0:T(8,128)S(1)} custom-call(f32[2560,128]{1,0:T(8,128)S(1)} %bitcast.35, bf16[1792,256]{1,0:T(8,128)(2,1)S(1)} %copy-done), custom_call_target="tpu_custom_call" | custom-call | tf_op jit(solution)/shard_map/pallas_call | solution.py:271
  69.0 1.1 %all-to-all-done.1.dh_hbm = f32[4,128,128]{2,1,0:T(8,128)} async-done(((f32[4,128,128]{2,1,0:T(8,128)}), f32[4,128,128]{2,1,0:T(8,128)}, u32[]{:S(2)}, u32[]{:S(2)}) %all-to-all-start.1) | async-done | bytes 262176 | tf_op jit(solution)/shard_map/all_to_all | solution.py:337
  70.1 1.0 shard_map.87
  71.1 0.0 copy-start.1
  71.1 0.0 copy-start.2
  71.1 40.5 %all_to_all.24 = f32[128,1,2176]{2,1,0:T(1,128)S(1)} all-to-all(f32[128,1,2176]{2,1,0:T(1,128)S(1)} %bitcast.38), channel_id=1, replica_groups={{0,76,152,228,304,380,456,20,96,172,248,324,400,476,40,116,192,268,344,..., dimensions={0} | all-to-all | bytes 2228224 | tf_op jit(solution)/shard_map/all_to_all | solution.py:287
  111.6 0.0 copy-done.1
  111.6 0.0 copy-done.2
  111.6 1.2 %shard_map.88 = (bf16[1024,128]{1,0:T(8,128)(2,1)}, bf16[1024,128]{1,0:T(8,128)(2,1)}, bf16[1024,128]{1,0:T(8,128)(2,1)}, bf16[128,128]{1,0:T(8,128)(2,1)}) custom-call(f32[2176,128]{1,0:T(8,128)S(1)} %bitcast.37, bf16[1024,128]{1,0:T(8,128)(2,1)S(1)} %bitcast.40, bf16[1024,128]{1,0:T(8,128)(2,1)S(1)} %bitcast.42), custom_call_target="tpu_custom_call" | custom-call | tf_op jit(solution)/shard_map/pallas_call | solution.py:271
Async XLA Ops:
  2.2 55.5 %copy-start = (bf16[1792,256]{1,0:T(8,128)(2,1)S(1)}, bf16[1792,256]{1,0:T(8,128)(2,1)}, u32[]{:S(2)}) copy-start(bf16[1792,256]{1,0:T(8,128)(2,1)} %constant.2.clone.refs_1_.table_ref) | copy-start | bytes 2752516
  60.4 9.7 %all-to-all-start.1 = ((f32[4,128,128]{2,1,0:T(8,128)}), f32[4,128,128]{2,1,0:T(8,128)}, u32[]{:S(2)}, u32[]{:S(2)}) async-start(f32[4,128,128]{2,1,0:T(8,128)} %shard_map.85), calls=%async_computation.1 | async-start | bytes 524288 | tf_op jit(solution)/shard_map/all_to_all | solution.py:337
  71.1 40.5 %copy-start.1 = (bf16[128,2,512]{2,1,0:T(2,128)(2,1)S(1)}, bf16[128,2,512]{2,1,0:T(2,128)(2,1)}, u32[]{:S(2)}) copy-start(bf16[128,2,512]{2,1,0:T(2,128)(2,1)} %param.5) | copy-start | bytes 786436
  71.1 40.5 %copy-start.2 = (bf16[128,2,512]{2,1,0:T(2,128)(2,1)S(1)}, bf16[128,2,512]{2,1,0:T(2,128)(2,1)}, u32[]{:S(2)}) copy-start(bf16[128,2,512]{2,1,0:T(2,128)(2,1)} %param.8) | copy-start | bytes 786436

commit v6 on v5

--- a/solution.py
+++ b/solution.py
@@ -13,7 +13,7 @@
 VMEM = pl.BlockSpec(memory_space=pltpu.VMEM)
 HBM = pl.BlockSpec(memory_space=pltpu.HBM)
 MIB = 1024 * 1024
-STRIDE = 19
+STRIDE = 1
 LATE = 1
 
 

time: 113 us -> 112 us (level)
  blocking collectives: 96 us -> 94.7 us
    all_to_all x2, blocking collectives: 96 us -> 94.7 us  [exchange(): lax.all_to_all(flat, 'seq', split_axis=0, concat_axis=0, axis_index_group...]
where the time goes in v6:
time: 112 us
  blocking collectives  94.7 us (85%)
  Pallas kernels  11 us (10%)
  starting transfers between devices  4.04 us (4%)
  waiting for transfers between devices  1.33 us (1%)
    all_to_all x2, blocking collectives, exchange(): lax.all_to_all(flat, 'seq', split_axis=0, concat_axis=0, axis_index_group...  94.7 us
    pallas_call x5, Pallas kernels, call(): pl.pallas_call(body, out_shape=outs, in_specs=spaces or [VMEM] * len(args...  11 us
    all_to_all x1, starting transfers between devices, per_device(): dh = lax.all_to_all(dh, 'ch', split_axis=0, concat_axis=0, tiled=True)  4.04 us
  transfers between devices with their start and end apart: 1, of which 1 were waited for; matrix products, arithmetic and copies ran while one was open for 0% of the time, Pallas kernels for 4%

profile of v6, /device:TPU:1, one launch (start us, length us, event | category | flops | bytes accessed | tf_op | source)
XLA Modules:
  0.0 111.7 jit_solution(7561244665725095725)
XLA Ops:
  0.6 1.6 %shard_map.84 = f32[2560,128]{1,0:T(8,128)S(1)} custom-call(bf16[1024,128]{1,0:T(8,128)(2,1)} %bitcast.39, bf16[1024,128]{1,0:T(8,128)(2,1)} %bitcast.43, bf16[1024,128]{1,0:T(8,128)(2,1)} %bitcast.41, bf16[128,512]{1,0:T(8,128)(2,1)} %refs_3_.1), custom_call_target="tpu_custom_call" | custom-call | tf_op jit(solution)/shard_map/pallas_call | solution.py:271
  2.2 0.0 copy-start
  2.3 54.4 %all_to_all.23 = f32[128,1,2560]{2,1,0:T(1,128)S(1)} all-to-all(f32[128,1,2560]{2,1,0:T(1,128)S(1)} %bitcast.36), channel_id=1, replica_groups={{0,4,8,12,16,20,24,28,32,36,40,44,48,52,56,60,64,68,72,76,80,84,88,92,9..., dimensions={0} | all-to-all | bytes 2621440 | tf_op jit(solution)/shard_map/all_to_all | solution.py:287
  56.7 0.0 copy-done
  56.7 2.7 %shard_map.85 = f32[4,128,128]{2,1,0:T(8,128)} custom-call(f32[2560,128]{1,0:T(8,128)S(1)} %bitcast.34, bf16[1792,256]{1,0:T(8,128)(2,1)S(1)} %copy-done), custom_call_target="tpu_custom_call" | custom-call | tf_op jit(solution)/shard_map/pallas_call | solution.py:271
  59.3 4.0 %all-to-all-start.1 = ((f32[4,128,128]{2,1,0:T(8,128)}), f32[4,128,128]{2,1,0:T(8,128)}, u32[]{:S(2)}, u32[]{:S(2)}) async-start(f32[4,128,128]{2,1,0:T(8,128)} %shard_map.85), calls=%async_computation.1 | async-start | bytes 524288 | tf_op jit(solution)/shard_map/all_to_all | solution.py:337
  63.4 4.5 %shard_map.86.big_ref = f32[2432,128]{1,0:T(8,128)S(1)} custom-call(f32[2560,128]{1,0:T(8,128)S(1)} %bitcast.35, bf16[1792,256]{1,0:T(8,128)(2,1)S(1)} %copy-done), custom_call_target="tpu_custom_call" | custom-call | tf_op jit(solution)/shard_map/pallas_call | solution.py:271
  67.9 1.3 %all-to-all-done.1.dh_hbm = f32[4,128,128]{2,1,0:T(8,128)} async-done(((f32[4,128,128]{2,1,0:T(8,128)}), f32[4,128,128]{2,1,0:T(8,128)}, u32[]{:S(2)}, u32[]{:S(2)}) %all-to-all-start.1) | async-done | bytes 262176 | tf_op jit(solution)/shard_map/all_to_all | solution.py:337
  69.2 1.0 shard_map.87
  70.2 0.0 copy-start.1
  70.2 0.0 copy-start.2
  70.2 40.3 %all_to_all.24 = f32[128,1,2176]{2,1,0:T(1,128)S(1)} all-to-all(f32[128,1,2176]{2,1,0:T(1,128)S(1)} %bitcast.38), channel_id=1, replica_groups={{0,4,8,12,16,20,24,28,32,36,40,44,48,52,56,60,64,68,72,76,80,84,88,92,9..., dimensions={0} | all-to-all | bytes 2228224 | tf_op jit(solution)/shard_map/all_to_all | solution.py:287
  110.6 0.0 copy-done.1
  110.6 0.0 copy-done.2
  110.6 1.2 %shard_map.88 = (bf16[1024,128]{1,0:T(8,128)(2,1)}, bf16[1024,128]{1,0:T(8,128)(2,1)}, bf16[1024,128]{1,0:T(8,128)(2,1)}, bf16[128,128]{1,0:T(8,128)(2,1)}) custom-call(f32[2176,128]{1,0:T(8,128)S(1)} %bitcast.37, bf16[1024,128]{1,0:T(8,128)(2,1)S(1)} %bitcast.40, bf16[1024,128]{1,0:T(8,128)(2,1)S(1)} %bitcast.42), custom_call_target="tpu_custom_call" | custom-call | tf_op jit(solution)/shard_map/pallas_call | solution.py:271
Async XLA Ops:
  2.2 54.4 %copy-start = (bf16[1792,256]{1,0:T(8,128)(2,1)S(1)}, bf16[1792,256]{1,0:T(8,128)(2,1)}, u32[]{:S(2)}) copy-start(bf16[1792,256]{1,0:T(8,128)(2,1)} %constant.2.clone.refs_1_.table_ref) | copy-start | bytes 2752516
  59.3 9.9 %all-to-all-start.1 = ((f32[4,128,128]{2,1,0:T(8,128)}), f32[4,128,128]{2,1,0:T(8,128)}, u32[]{:S(2)}, u32[]{:S(2)}) async-start(f32[4,128,128]{2,1,0:T(8,128)} %shard_map.85), calls=%async_computation.1 | async-start | bytes 524288 | tf_op jit(solution)/shard_map/all_to_all | solution.py:337
  70.2 40.3 %copy-start.1 = (bf16[128,2,512]{2,1,0:T(2,128)(2,1)S(1)}, bf16[128,2,512]{2,1,0:T(2,128)(2,1)}, u32[]{:S(2)}) copy-start(bf16[128,2,512]{2,1,0:T(2,128)(2,1)} %param.5) | copy-start | bytes 786436
  70.2 40.3 %copy-start.2 = (bf16[128,2,512]{2,1,0:T(2,128)(2,1)S(1)}, bf16[128,2,512]{2,1,0:T(2,128)(2,1)}, u32[]{:S(2)}) copy-start(bf16[128,2,512]{2,1,0:T(2,128)(2,1)} %param.8) | copy-start | bytes 786436

commit v7 on v6

--- a/solution.py
+++ b/solution.py
@@ -13,7 +13,6 @@
 VMEM = pl.BlockSpec(memory_space=pltpu.VMEM)
 HBM = pl.BlockSpec(memory_space=pltpu.HBM)
 MIB = 1024 * 1024
-STRIDE = 1
 LATE = 1
 
 
@@ -295,7 +294,9 @@
     blocks = lax.axis_size("seq")
     parts = filters // blocks
     width = group * parts
-    order = [STRIDE * i % blocks for i in range(blocks)]
+    side = math.isqrt(blocks // 2)
+    grid = np.arange(blocks).reshape(blocks // (2 * side), side, 2)
+    order = [int(i) for i in grid.transpose(1, 0, 2).reshape(-1)]
     tables = make_tables(rows, blocks, order)
 
     def to_rows(x):

time: 112 us -> 112 us (level)
  no operation moved by 1% of the time
where the time goes in v7:
time: 112 us; the launch traced here: 111 us
  blocking collectives  94.5 us (84%)
  Pallas kernels  11 us (10%)
  starting transfers between devices  4.04 us (4%)
    all_to_all x2, blocking collectives, exchange(): lax.all_to_all(flat, 'seq', split_axis=0, concat_axis=0, axis_index_group...  94.5 us
    pallas_call x5, Pallas kernels, call(): pl.pallas_call(body, out_shape=outs, in_specs=spaces or [VMEM] * len(args...  11 us
    all_to_all x1, starting transfers between devices, per_device(): dh = lax.all_to_all(dh, 'ch', split_axis=0, concat_axis=0, tiled=True)  4.04 us
  transfers between devices with their start and end apart: 1, of which 1 were waited for; matrix products, arithmetic and copies ran while one was open for 0% of the time, Pallas kernels for 4%

profile of v7, /device:TPU:1, one launch (start us, length us, event | category | flops | bytes accessed | tf_op | source)
XLA Modules:
  0.0 111.3 jit_solution(3168798582243497532)
XLA Ops:
  0.6 1.6 %shard_map.84 = f32[2560,128]{1,0:T(8,128)S(1)} custom-call(bf16[1024,128]{1,0:T(8,128)(2,1)} %bitcast.39, bf16[1024,128]{1,0:T(8,128)(2,1)} %bitcast.43, bf16[1024,128]{1,0:T(8,128)(2,1)} %bitcast.41, bf16[128,512]{1,0:T(8,128)(2,1)} %refs_3_.1), custom_call_target="tpu_custom_call" | custom-call | tf_op jit(solution)/shard_map/pallas_call | solution.py:270
  2.2 0.0 copy-start
  2.3 53.9 %all_to_all.23 = f32[128,1,2560]{2,1,0:T(1,128)S(1)} all-to-all(f32[128,1,2560]{2,1,0:T(1,128)S(1)} %bitcast.36), channel_id=1, replica_groups={{0,4,64,68,128,132,192,196,256,260,320,324,384,388,448,452,8,12,72,76,1..., dimensions={0} | all-to-all | bytes 2621440 | tf_op jit(solution)/shard_map/all_to_all | solution.py:286
  56.2 0.0 copy-done
  56.2 2.7 %shard_map.85 = f32[4,128,128]{2,1,0:T(8,128)} custom-call(f32[2560,128]{1,0:T(8,128)S(1)} %bitcast.34, bf16[1792,256]{1,0:T(8,128)(2,1)S(1)} %copy-done), custom_call_target="tpu_custom_call" | custom-call | tf_op jit(solution)/shard_map/pallas_call | solution.py:270
  58.9 4.0 %all-to-all-start.1 = ((f32[4,128,128]{2,1,0:T(8,128)}), f32[4,128,128]{2,1,0:T(8,128)}, u32[]{:S(2)}, u32[]{:S(2)}) async-start(f32[4,128,128]{2,1,0:T(8,128)} %shard_map.85), calls=%async_computation.1 | async-start | bytes 524288 | tf_op jit(solution)/shard_map/all_to_all | solution.py:338
  62.9 4.5 %shard_map.86.big_ref = f32[2432,128]{1,0:T(8,128)S(1)} custom-call(f32[2560,128]{1,0:T(8,128)S(1)} %bitcast.35, bf16[1792,256]{1,0:T(8,128)(2,1)S(1)} %copy-done), custom_call_target="tpu_custom_call" | custom-call | tf_op jit(solution)/shard_map/pallas_call | solution.py:270
  67.4 1.1 all-to-all-done.1.dh_hbm
  68.5 1.0 shard_map.87
  69.5 0.0 copy-start.1
  69.5 0.0 copy-start.2
  69.5 40.6 %all_to_all.24 = f32[128,1,2176]{2,1,0:T(1,128)S(1)} all-to-all(f32[128,1,2176]{2,1,0:T(1,128)S(1)} %bitcast.38), channel_id=1, replica_groups={{0,4,64,68,128,132,192,196,256,260,320,324,384,388,448,452,8,12,72,76,1..., dimensions={0} | all-to-all | bytes 2228224 | tf_op jit(solution)/shard_map/all_to_all | solution.py:286
  110.1 0.0 copy-done.1
  110.1 0.0 copy-done.2
  110.1 1.2 %shard_map.88 = (bf16[1024,128]{1,0:T(8,128)(2,1)}, bf16[1024,128]{1,0:T(8,128)(2,1)}, bf16[1024,128]{1,0:T(8,128)(2,1)}, bf16[128,128]{1,0:T(8,128)(2,1)}) custom-call(f32[2176,128]{1,0:T(8,128)S(1)} %bitcast.37, bf16[1024,128]{1,0:T(8,128)(2,1)S(1)} %bitcast.40, bf16[1024,128]{1,0:T(8,128)(2,1)S(1)} %bitcast.42), custom_call_target="tpu_custom_call" | custom-call | tf_op jit(solution)/shard_map/pallas_call | solution.py:270
Async XLA Ops:
  2.2 53.9 %copy-start = (bf16[1792,256]{1,0:T(8,128)(2,1)S(1)}, bf16[1792,256]{1,0:T(8,128)(2,1)}, u32[]{:S(2)}) copy-start(bf16[1792,256]{1,0:T(8,128)(2,1)} %constant.2.clone.refs_1_.table_ref) | copy-start | bytes 2752516
  58.9 9.6 %all-to-all-start.1 = ((f32[4,128,128]{2,1,0:T(8,128)}), f32[4,128,128]{2,1,0:T(8,128)}, u32[]{:S(2)}, u32[]{:S(2)}) async-start(f32[4,128,128]{2,1,0:T(8,128)} %shard_map.85), calls=%async_computation.1 | async-start | bytes 524288 | tf_op jit(solution)/shard_map/all_to_all | solution.py:338
  69.5 40.6 %copy-start.1 = (bf16[128,2,512]{2,1,0:T(2,128)(2,1)S(1)}, bf16[128,2,512]{2,1,0:T(2,128)(2,1)}, u32[]{:S(2)}) copy-start(bf16[128,2,512]{2,1,0:T(2,128)(2,1)} %param.5) | copy-start | bytes 786436
  69.5 40.6 %copy-start.2 = (bf16[128,2,512]{2,1,0:T(2,128)(2,1)S(1)}, bf16[128,2,512]{2,1,0:T(2,128)(2,1)}, u32[]{:S(2)}) copy-start(bf16[128,2,512]{2,1,0:T(2,128)(2,1)} %param.8) | copy-start | bytes 786436

commit v8 on v7

--- a/solution.py
+++ b/solution.py
@@ -295,8 +295,8 @@
     parts = filters // blocks
     width = group * parts
     side = math.isqrt(blocks // 2)
-    grid = np.arange(blocks).reshape(blocks // (2 * side), side, 2)
-    order = [int(i) for i in grid.transpose(1, 0, 2).reshape(-1)]
+    z, y, core = np.arange(blocks) // (2 * side), np.arange(blocks) // 2 % side, np.arange(blocks) % 2
+    order = [int(i) for i in np.lexsort((y, core, (z - y) % side))]
     tables = make_tables(rows, blocks, order)
 
     def to_rows(x):

time: 112 us -> 114 us (1.018)
  waiting for transfers between devices: 1.07 us -> 2.29 us
    all_to_all x1, waiting for transfers between devices: 1.07 us -> 2.29 us  [per_device(): dh = lax.all_to_all(dh, 'ch', split_axis=0, concat_axis=0, tiled=True)]
where the time goes in v8:
time: 114 us
  blocking collectives  95.6 us (84%)
  Pallas kernels  11 us (10%)
  starting transfers between devices  4.04 us (4%)
  waiting for transfers between devices  2.29 us (2%)
    all_to_all x2, blocking collectives, exchange(): lax.all_to_all(flat, 'seq', split_axis=0, concat_axis=0, axis_index_group...  95.6 us
    pallas_call x5, Pallas kernels, call(): pl.pallas_call(body, out_shape=outs, in_specs=spaces or [VMEM] * len(args...  11 us
    all_to_all x1, starting transfers between devices, per_device(): dh = lax.all_to_all(dh, 'ch', split_axis=0, concat_axis=0, tiled=True)  4.04 us
    all_to_all x1, waiting for transfers between devices, per_device(): dh = lax.all_to_all(dh, 'ch', split_axis=0, concat_axis=0, tiled=True)  2.29 us
  transfers between devices with their start and end apart: 1, of which 1 were waited for; matrix products, arithmetic and copies ran while one was open for 0% of the time, Pallas kernels for 4%

profile of v8, /device:TPU:1, one launch (start us, length us, event | category | flops | bytes accessed | tf_op | source)
XLA Modules:
  0.0 113.6 jit_solution(15198768251871423109)
XLA Ops:
  0.6 1.6 %shard_map.84 = f32[2560,128]{1,0:T(8,128)S(1)} custom-call(bf16[1024,128]{1,0:T(8,128)(2,1)} %bitcast.39, bf16[1024,128]{1,0:T(8,128)(2,1)} %bitcast.43, bf16[1024,128]{1,0:T(8,128)(2,1)} %bitcast.41, bf16[128,512]{1,0:T(8,128)(2,1)} %refs_3_.1), custom_call_target="tpu_custom_call" | custom-call | tf_op jit(solution)/shard_map/pallas_call | solution.py:270
  2.2 0.0 copy-start
  2.3 56.6 %all_to_all.23 = f32[128,1,2560]{2,1,0:T(1,128)S(1)} all-to-all(f32[128,1,2560]{2,1,0:T(1,128)S(1)} %bitcast.36), channel_id=1, replica_groups={{0,72,144,216,288,360,432,504,4,76,148,220,292,364,436,508,64,136,208,2..., dimensions={0} | all-to-all | bytes 2621440 | tf_op jit(solution)/shard_map/all_to_all | solution.py:286
  58.8 0.0 copy-done
  58.8 2.7 %shard_map.85 = f32[4,128,128]{2,1,0:T(8,128)} custom-call(f32[2560,128]{1,0:T(8,128)S(1)} %bitcast.34, bf16[1792,256]{1,0:T(8,128)(2,1)S(1)} %copy-done), custom_call_target="tpu_custom_call" | custom-call | tf_op jit(solution)/shard_map/pallas_call | solution.py:270
  61.5 4.0 %all-to-all-start.1 = ((f32[4,128,128]{2,1,0:T(8,128)}), f32[4,128,128]{2,1,0:T(8,128)}, u32[]{:S(2)}, u32[]{:S(2)}) async-start(f32[4,128,128]{2,1,0:T(8,128)} %shard_map.85), calls=%async_computation.1 | async-start | bytes 524288 | tf_op jit(solution)/shard_map/all_to_all | solution.py:338
  65.6 4.5 %shard_map.86.big_ref = f32[2432,128]{1,0:T(8,128)S(1)} custom-call(f32[2560,128]{1,0:T(8,128)S(1)} %bitcast.35, bf16[1792,256]{1,0:T(8,128)(2,1)S(1)} %copy-done), custom_call_target="tpu_custom_call" | custom-call | tf_op jit(solution)/shard_map/pallas_call | solution.py:270
  70.1 2.3 %all-to-all-done.1.dh_hbm = f32[4,128,128]{2,1,0:T(8,128)} async-done(((f32[4,128,128]{2,1,0:T(8,128)}), f32[4,128,128]{2,1,0:T(8,128)}, u32[]{:S(2)}, u32[]{:S(2)}) %all-to-all-start.1) | async-done | bytes 262176 | tf_op jit(solution)/shard_map/all_to_all | solution.py:338
  72.4 1.0 shard_map.87
  73.4 0.0 copy-start.1
  73.4 0.0 copy-start.2
  73.4 39.0 %all_to_all.24 = f32[128,1,2176]{2,1,0:T(1,128)S(1)} all-to-all(f32[128,1,2176]{2,1,0:T(1,128)S(1)} %bitcast.38), channel_id=1, replica_groups={{0,72,144,216,288,360,432,504,4,76,148,220,292,364,436,508,64,136,208,2..., dimensions={0} | all-to-all | bytes 2228224 | tf_op jit(solution)/shard_map/all_to_all | solution.py:286
  112.4 0.0 copy-done.1
  112.4 0.0 copy-done.2
  112.4 1.2 %shard_map.88 = (bf16[1024,128]{1,0:T(8,128)(2,1)}, bf16[1024,128]{1,0:T(8,128)(2,1)}, bf16[1024,128]{1,0:T(8,128)(2,1)}, bf16[128,128]{1,0:T(8,128)(2,1)}) custom-call(f32[2176,128]{1,0:T(8,128)S(1)} %bitcast.37, bf16[1024,128]{1,0:T(8,128)(2,1)S(1)} %bitcast.40, bf16[1024,128]{1,0:T(8,128)(2,1)S(1)} %bitcast.42), custom_call_target="tpu_custom_call" | custom-call | tf_op jit(solution)/shard_map/pallas_call | solution.py:270
Async XLA Ops:
  2.2 56.6 %copy-start = (bf16[1792,256]{1,0:T(8,128)(2,1)S(1)}, bf16[1792,256]{1,0:T(8,128)(2,1)}, u32[]{:S(2)}) copy-start(bf16[1792,256]{1,0:T(8,128)(2,1)} %constant.2.clone.refs_1_.table_ref) | copy-start | bytes 2752516
  61.5 10.9 %all-to-all-start.1 = ((f32[4,128,128]{2,1,0:T(8,128)}), f32[4,128,128]{2,1,0:T(8,128)}, u32[]{:S(2)}, u32[]{:S(2)}) async-start(f32[4,128,128]{2,1,0:T(8,128)} %shard_map.85), calls=%async_computation.1 | async-start | bytes 524288 | tf_op jit(solution)/shard_map/all_to_all | solution.py:338
  73.4 39.1 %copy-start.1 = (bf16[128,2,512]{2,1,0:T(2,128)(2,1)S(1)}, bf16[128,2,512]{2,1,0:T(2,128)(2,1)}, u32[]{:S(2)}) copy-start(bf16[128,2,512]{2,1,0:T(2,128)(2,1)} %param.5) | copy-start | bytes 786436
  73.4 39.0 %copy-start.2 = (bf16[128,2,512]{2,1,0:T(2,128)(2,1)S(1)}, bf16[128,2,512]{2,1,0:T(2,128)(2,1)}, u32[]{:S(2)}) copy-start(bf16[128,2,512]{2,1,0:T(2,128)(2,1)} %param.8) | copy-start | bytes 786436
